TPU v7x, 256 devices: a whole 4x4x8 slice. The times are simulated.
256 devices in a mesh: gx: 4 (over y_lo, core), gy: 4 (over x), gz: 16 (over y_hi, z).
Axes of the slice: x: 4, y: 4 (y_hi: 2, y_lo: 2; y = y_hi * 2 + y_lo), z: 8, core: 2. Of those that a mesh axis runs over, the one named last changes fastest.
Arguments:
- permeability: float32 [512, 64, 512], P('gz', 'gx', 'gy'), may hold values from 0.1 to 10
- accumulation: float32 [512, 64, 512], P('gz', 'gx', 'gy'), may hold values from 0.0001 to 0.001
- source_term: float32 [512, 64, 512], P('gz', 'gx', 'gy'), may hold values from -1.6 to 1.6
- vertical_trans: float32 [512, 64, 512], P('gz', 'gx', 'gy'), may hold values from 0.05 to 0.5
Outputs:
- pressure: float32 [512, 64, 512], P('gz', 'gx', 'gy')
- residual: float32 [512, 64, 512], P('gz', 'gx', 'gy')
All inputs are finite; a program needn't handle non-finite values.
Results may differ from a plain program's by a relative error of at most 0.0003.
Values sent between devices are 32-bit elements; how exact they have to be, the bound alone decides.
A program may use at most 64 MiB of HBM per device.

v0:
```python
import jax
import jax.numpy as jnp
from jax import lax
from jax.experimental import pallas as pl
from jax.experimental.pallas import tpu as pltpu
from jax.sharding import PartitionSpec as P

SWEEPS = 8
LAYERS = 32
SIDE = 4
DEPTH = 16
DUALS = 9
MESH = pl.DeviceIdType.MESH
F32 = jnp.float32
LX, LY, LXY = 0, 1, 2


def lane_roll(value, groups):
    by = (groups * 32) % 128
    return value if by == 0 else pltpu.roll(value, by, axis=1)


def sub_roll(value, by):
    return pltpu.roll(value, by % 8, axis=0)


def inverse(value):
    guess = pl.reciprocal(value, approx=True)
    guess = guess * (2.0 - value * guess)
    return guess * (2.0 - value * guess)


def harmonic(left, right):
    return 2.0 * left * right * inverse(left + right)


def node_shift(value, by, row):
    if by % 8 == 0:
        return lane_roll(value, -(by // 8))
    turned = sub_roll(value, -by)
    if by > 0:
        return jnp.where(row < 8 - by, turned, lane_roll(turned, -1))
    return jnp.where(row >= -by, turned, lane_roll(turned, 1))


def factor(b):
    low = {}
    inv = [None] * 4
    for k in range(4):
        pivot = b[(k, k)]
        for m in range(k):
            if low.get((k, m)) is not None:
                pivot = pivot - low[(k, m)] * work[(k, m)]
        inv[k] = inverse(pivot)
        if k == 0:
            work = {}
        for i in range(k + 1, 4):
            entry = b[(i, k)]
            for m in range(k):
                if low.get((i, m)) is None or work.get((k, m)) is None:
                    continue
                term = low[(i, m)] * work[(k, m)]
                entry = -term if entry is None else entry - term
            work[(i, k)] = entry
            low[(i, k)] = None if entry is None else entry * inv[k]
    return low, inv


def forward(low, column):
    out = []
    for i in range(4):
        value = column[i]
        for m in range(i):
            if low[(i, m)] is not None and out[m] is not None:
                term = low[(i, m)] * out[m]
                value = -term if value is None else value - term
        out.append(value)
    return out


def scaled(inv, column):
    return [None if v is None else v * inv[k] for k, v in enumerate(column)]


def inner(left, right):
    total = None
    for a, b in zip(left, right):
        if a is None or b is None:
            continue
        total = a * b if total is None else total + a * b
    return total


def subtract(value, term):
    if term is None:
        return value
    return -term if value is None else value - term


def shift_or_none(value, by, row):
    return None if value is None else node_shift(value, by, row)


def solve_nodes(b, c, d, row):
    for step in (1, 2, 4, 8):
        a = [[shift_or_none(c[m][k], -step, row) for m in range(4)] for k in range(4)]
        low, inv = factor(b)
        up = [forward(low, [c[i][k] for i in range(4)]) for k in range(4)]
        down = [forward(low, [a[i][k] for i in range(4)]) for k in range(4)]
        side = scaled(inv, forward(low, d))
        up_s = [scaled(inv, col) for col in up]
        down_s = [scaled(inv, col) for col in down]
        new_b = {}
        for i in range(4):
            for k in range(i + 1):
                value = subtract(b[(i, k)], shift_or_none(inner(up[i], up_s[k]), -step, row))
                new_b[(i, k)] = subtract(value, shift_or_none(inner(down[i], down_s[k]), step, row))
        new_d = []
        for i in range(4):
            value = subtract(d[i], shift_or_none(inner(up[i], side), -step, row))
            new_d.append(subtract(value, shift_or_none(inner(down[i], side), step, row)))
        new_c = [
            [subtract(None, shift_or_none(inner(down[i], up_s[k]), step, row)) for k in range(4)]
            for i in range(4)
        ]
        b, c, d = new_b, new_c, new_d
    both = [[c[i][k] + node_shift(c[k][i], -16, row) for k in range(4)] for i in range(4)]
    low, inv = factor(b)
    cols = [forward(low, [both[i][k] for i in range(4)]) for k in range(4)]
    cols_s = [scaled(inv, col) for col in cols]
    side = scaled(inv, forward(low, d))
    last = {}
    for i in range(4):
        for k in range(i + 1):
            last[(i, k)] = b[(i, k)] - node_shift(inner(cols[i], cols_s[k]), 16, row)
    right = [d[i] - node_shift(inner(cols[i], side), 16, row) for i in range(4)]
    low, inv = factor(last)
    value = scaled(inv, forward(low, right))
    for i in (2, 1, 0):
        for k in range(i + 1, 4):
            value[i] = value[i] - low[(k, i)] * value[k]
    return value


def corner_sums(g, r):
    k = [
        g[(3, 3)],
        g[(2, 3)] - g[(3, 3)],
        g[(1, 3)] - g[(3, 3)],
        g[(0, 3)] - g[(1, 3)] - g[(2, 3)] + g[(3, 3)],
        g[(2, 2)] - 2.0 * g[(2, 3)] + g[(3, 3)],
        g[(1, 2)] - g[(1, 3)] - g[(2, 3)] + g[(3, 3)],
        (g[(0, 2)] - g[(1, 2)] - g[(2, 2)]) + (2.0 * g[(2, 3)] - g[(0, 3)] + g[(1, 3)] - g[(3, 3)]),
        g[(1, 1)] - 2.0 * g[(1, 3)] + g[(3, 3)],
        (g[(0, 1)] - g[(1, 1)] - g[(1, 2)]) + (2.0 * g[(1, 3)] - g[(0, 3)] + g[(2, 3)] - g[(3, 3)]),
        (g[(0, 0)] + g[(1, 1)] + g[(2, 2)] + g[(3, 3)])
        - 2.0 * (g[(0, 1)] + g[(0, 2)] + g[(1, 3)] + g[(2, 3)] - g[(0, 3)] - g[(1, 2)]),
        r[3],
        r[2] - r[3],
        r[1] - r[3],
        r[0] - r[1] - r[2] + r[3],
    ]
    return k


GRAM = ((0, 0), (0, 1), (0, 2), (0, 3), (1, 1), (1, 2), (1, 3), (2, 2), (2, 3), (3, 3))


def assemble(t, row):
    def back(value):
        return node_shift(value, -1, row)

    b, d = {}, []
    c = [[None] * 4 for _ in range(4)]
    for i in range(4):
        w = (i - 1) % 4
        b[(i, i)] = t[0][i] + t[4][w] + back(t[7][i] + t[9][w])
        d.append(t[10][i] + t[11][w] + back(t[12][i] + t[13][w]))
        edge = t[1][i] + back(t[8][i])
        e = (i + 1) % 4
        b[(max(i, e), min(i, e))] = edge
        c[i][i] = t[2][i] + t[6][w]
        c[i][e] = t[3][i]
        c[e][i] = t[5][i]
    b[(2, 0)] = None
    b[(3, 1)] = None
    return b, c, d


def kernel(
    perm, accum, source, vtrans, press_out, resid_out,
    hx, ax, sx, vt, row24, row8, tp, at, st, te, tn, co, bf, sums, ga, nodes, cb, pt, py, ry, fp, po, ro,
    up_layer, down_pair,
    local_sem, send_sem, recv_sem, gsend_sem, grecv_sem, out_sem,
):
    gx, gy, gz = lax.axis_index("gx"), lax.axis_index("gy"), lax.axis_index("gz")

    def peer(dx, dy, dz):
        return (
            lax.rem(gx + (dx + SIDE), SIDE),
            lax.rem(gy + (dy + SIDE), SIDE),
            lax.rem(gz + (dz + DEPTH), DEPTH),
        )

    local = [
        pltpu.make_async_copy(perm.at[:, 0], hx.at[1], local_sem.at[0]),
        pltpu.make_async_copy(perm.at[:, 1], hx.at[2], local_sem.at[1]),
        pltpu.make_async_copy(accum.at[:, 0], ax.at[1], local_sem.at[2]),
        pltpu.make_async_copy(accum.at[:, 1], ax.at[2], local_sem.at[3]),
        pltpu.make_async_copy(source.at[:, 0], sx.at[1], local_sem.at[4]),
        pltpu.make_async_copy(source.at[:, 1], sx.at[2], local_sem.at[5]),
        pltpu.make_async_copy(vtrans, vt, local_sem.at[6]),
    ]
    for copy in local:
        copy.start()

    barrier = pltpu.get_barrier_semaphore()
    for dx in range(SIDE):
        for dy in range(SIDE):
            if dx or dy:
                pl.semaphore_signal(barrier, inc=1, device_id=peer(dx, dy, 0), device_id_type=MESH)
    for dz in (-1, 1):
        pl.semaphore_signal(barrier, inc=1, device_id=peer(0, 0, dz), device_id_type=MESH)
    pl.semaphore_wait(barrier, 17)

    def remote(src, dst, at_sem, target):
        return pltpu.make_async_remote_copy(
            src_ref=src, dst_ref=dst, send_sem=send_sem.at[at_sem], recv_sem=recv_sem.at[at_sem],
            device_id=target, device_id_type=MESH,
        )

    west, east = peer(-1, 0, 0), peer(1, 0, 0)
    south, north = peer(0, -1, 0), peer(0, 1, 0)
    perm_w = remote(perm.at[:, 0], hx.at[3], 0, west)
    perm_e = remote(perm.at[:, 1], hx.at[0], 1, east)
    perm_w.start()
    perm_e.start()
    for copy in local[:2]:
        copy.wait()
    hx_rows = hx.reshape(4 * 256, 128)
    ax_rows = ax.reshape(4 * 256, 128)
    sx_rows = sx.reshape(4 * 256, 128)
    row8[...] = hx_rows[pl.ds(512, LAYERS, stride=8), :]
    perm_r = remote(row8, row24, 2, west)
    perm_r.start()
    accum_w = remote(accum.at[:, 0], ax.at[3], 3, west)
    source_w = remote(source.at[:, 0], sx.at[3], 4, west)
    accum_w.start()
    source_w.start()
    for copy in local[2:]:
        copy.wait()
    vt_up = remote(vt.at[pl.ds(496, 16)], down_pair.at[1], 5, peer(0, 0, 1))
    vt_up.start()

    row = lax.broadcasted_iota(jnp.int32, (8, 128), 0)
    lane = lax.broadcasted_iota(jnp.int32, (8, 128), 1)
    group = lane // 32
    u_base = jnp.where(group % 2 == 1, 8, 0)
    row0 = row == 0
    row7 = row == 7
    u0 = u_base == 0
    u8 = u_base == 8

    perm_w.wait()
    perm_e.wait()
    perm_r.wait()
    for x in range(8):
        tp[x, pl.ds(8, 128), :] = hx_rows[pl.ds(x, 128, stride=8), :].T
    tp[8, pl.ds(8, 128), :] = jnp.concatenate(
        [hx_rows[pl.ds(256, 96, stride=8), :], row24[...]], axis=0
    ).T
    strip_s = remote(tp.at[:, pl.ds(8, 16), :], tp.at[:, pl.ds(136, 16), :], 6, south)
    strip_n = remote(tp.at[:, pl.ds(128, 8), :], tp.at[:, pl.ds(0, 8), :], 7, north)
    strip_s.start()
    strip_n.start()
    accum_s = remote(at.at[:, pl.ds(8, 8), :], at.at[:, pl.ds(136, 8), :], 8, south)
    source_s = remote(st.at[:, pl.ds(8, 8), :], st.at[:, pl.ds(136, 8), :], 9, south)

    def relax(k, carry):
        d = lax.rem(k + 1, DUALS)

        @pl.when(k == 3)
        def _():
            accum_w.wait()
            source_w.wait()
            for x in range(8):
                at[x, pl.ds(8, 128), :] = ax_rows[pl.ds(x, 128, stride=8), :].T
                st[x, pl.ds(8, 128), :] = sx_rows[pl.ds(x, 128, stride=8), :].T
            accum_s.start()
            source_s.start()

        @pl.when(k == 7)
        def _():
            strip_s.wait()
            strip_n.wait()

        cells = [[tp[x, pl.ds(16 * d + p, 8, stride=2), :] for p in range(2)] for x in range(9)]
        t_e = [[harmonic(cells[x][p], cells[x + 1][p]) for p in range(2)] for x in range(8)]
        for x in range(8):
            after = tp[x, pl.ds(16 * d + 2, 8, stride=2), :]
            t_n = [harmonic(cells[x][0], cells[x][1]), harmonic(cells[x][1], after)]
            t_s = [sub_roll(t_n[1], 1), t_n[0]]
            for p in range(2):
                t_w = t_e[x - 1][p] if x else lane_roll(t_e[7][p], 1)
                te[d, x, p] = t_e[x][p]
                tn[d, x, p] = t_n[p]
                inv = inverse((t_w + t_e[x][p]) + (t_s[p] + t_n[p]))
                co[0, x, p] = t_w * inv
                co[1, x, p] = t_e[x][p] * inv
                co[2, x, p] = t_s[p] * inv
                co[3, x, p] = t_n[p] * inv
            co[4, x, 0] = jnp.where(row7, 0.0, co[3, x, 1])
        co[4, 0, 1] = jnp.where(u8, 0.0, co[1, 7, 0])
        co[4, 1, 1] = jnp.where(u8, 0.0, co[1, 7, 1])

        fixed = [[row0 | u0, u0]] + [[row0, None]] * 7
        for kind in range(3):
            vals = []
            for x in range(8):
                along_x = 1.0 - (u_base + x).astype(F32) / 16.0
                pair = []
                for p in range(2):
                    along_y = 1.0 - (2 * row + p).astype(F32) / 16.0
                    pair.append((along_x, along_y, along_x * along_y)[kind])
                vals.append(pair)
            for _ in range(SWEEPS):
                new = []
                for x in range(8):
                    pair = []
                    for p in range(2):
                        west_v = vals[x - 1][p] if x else lane_roll(vals[7][p], 1)
                        east_v = vals[x + 1][p] if x < 7 else lane_roll(vals[0][p], -1)
                        south_v = vals[x][0] if p else sub_roll(vals[x][1], 1)
                        north_v = sub_roll(vals[x][0], -1) if p else vals[x][1]
                        c_e = co[4, p, 1] if x == 7 and kind != LY else co[1, x, p]
                        c_n = co[4, x, 0] if p and kind != LX else co[3, x, p]
                        value = (co[0, x, p] * west_v + c_e * east_v) + (co[2, x, p] * south_v + c_n * north_v)
                        keep = fixed[x][p]
                        pair.append(value if keep is None else jnp.where(keep, vals[x][p], value))
                    new.append(pair)
                vals = new
            for x in range(8):
                for p in range(2):
                    bf[kind, d, x, p] = vals[x][p]
        return carry

    lax.fori_loop(0, DUALS, relax, 0)

    def gram(d, carry):
        @pl.when(d == 8)
        def _():
            accum_s.wait()
            source_s.wait()

        acc = {}

        def add(key, value):
            acc[key] = value if key not in acc else acc[key] + value

        for x in range(8):
            for p in range(2):
                a = at[x, pl.ds(16 * d + p, 8, stride=2), :]
                s = st[x, pl.ds(16 * d + p, 8, stride=2), :]
                here = [bf[kind, d, x, p] for kind in range(3)]
                t_e, t_n = te[d, x, p], tn[d, x, p]
                mass, d_e, d_n = [], [], []
                for kind in range(3):
                    if x < 7:
                        east_v = bf[kind, d, x + 1, p]
                    else:
                        east_v = lane_roll(bf[kind, d, 0, p], -1)
                        if kind != LY:
                            east_v = jnp.where(u8, 0.0, east_v)
                    if p:
                        north_v = sub_roll(bf[kind, d, x, 0], -1)
                        if kind != LX:
                            north_v = jnp.where(row7, 0.0, north_v)
                    else:
                        north_v = bf[kind, d, x, 1]
                    d_e.append(here[kind] - east_v)
                    d_n.append(here[kind] - north_v)
                    mass.append(a * here[kind])
                add((0, 0), a)
                add("r0", s)
                for kind in range(3):
                    add((0, kind + 1), mass[kind])
                    add("r" + str(kind + 1), s * here[kind])
                    w_e, w_n = t_e * d_e[kind], t_n * d_n[kind]
                    for other in range(kind, 3):
                        add((kind + 1, other + 1), mass[kind] * here[other] + w_e * d_e[other] + w_n * d_n[other])
        mine = row == d - 1
        for index, key in enumerate(GRAM + ("r0", "r1", "r2", "r3")):
            value = acc[key]
            value = value + sub_roll(value, 4)
            value = value + sub_roll(value, 2)
            value = value + sub_roll(value, 1)
            sums[index] = jnp.where(mine, value, sums[index])
        return carry

    lax.fori_loop(1, DUALS, gram, 0)

    whole = []
    for index in range(14):
        value = sums[index]
        whole.append(value + lane_roll(value, -1))
    entries = corner_sums({key: whole[i] for i, key in enumerate(GRAM)}, whole[10:])
    for k in range(4):
        packed = jnp.zeros((8, 128), F32)
        for q in range(4):
            if 4 * k + q < 14:
                packed = jnp.where(group == q, lane_roll(entries[4 * k + q], q - 2), packed)
        ga[0, k] = packed
    gathers = []
    for dx in range(SIDE):
        for dy in range(SIDE):
            if dx or dy:
                slot = (-dx % SIDE) * SIDE + (-dy % SIDE)
                gathers.append(
                    pltpu.make_async_remote_copy(
                        src_ref=ga.at[0], dst_ref=ga.at[slot],
                        send_sem=gsend_sem.at[slot], recv_sem=grecv_sem.at[slot],
                        device_id=peer(dx, dy, 0), device_id_type=MESH,
                    )
                )
    for copy in gathers:
        copy.start()
    for copy in gathers:
        copy.wait()

    table = []
    for index in range(14):
        k, q = index // 4, index % 4
        by_x = []
        for i in range(SIDE):
            value = lane_roll(ga[i * SIDE, k], -q)
            for g in range(1, SIDE):
                value = jnp.where(group == g, lane_roll(ga[i * SIDE + g, k], g - q), value)
            by_x.append(value)
        table.append(by_x)
    b, c, d_side = assemble(table, row)
    coarse = solve_nodes(b, c, d_side, row)

    def everywhere(value, g):
        value = jnp.where(group == g, value, 0.0)
        value = value + lane_roll(value, 1)
        return value + lane_roll(value, 2)

    first_half = lane < 64
    for at_row, g in ((0, 3), (8, 0), (16, 1)):
        mid = everywhere(coarse[0], g)
        nodes[0, pl.ds(at_row, 8), :] = jnp.where(first_half, everywhere(coarse[3], g), mid)
        nodes[1, pl.ds(at_row, 8), :] = jnp.where(first_half, mid, everywhere(coarse[1], g))
    for d in range(DUALS):
        c0 = jnp.broadcast_to(nodes[0, pl.ds(7 + d, 1), :], (8, 128))
        c1 = jnp.broadcast_to(nodes[1, pl.ds(7 + d, 1), :], (8, 128))
        c2 = jnp.broadcast_to(nodes[0, pl.ds(8 + d, 1), :], (8, 128))
        c3 = jnp.broadcast_to(nodes[1, pl.ds(8 + d, 1), :], (8, 128))
        cb[d, 0] = c3
        cb[d, 1] = c2 - c3
        cb[d, 2] = c1 - c3
        cb[d, 3] = (c0 - c1) - (c2 - c3)

    def interpolate(d, carry):
        w = [cb[d, k] for k in range(4)]
        for x in range(8):
            for p in range(2):
                value = (w[0] + w[1] * bf[0, d, x, p]) + (w[2] * bf[1, d, x, p] + w[3] * bf[2, d, x, p])
                pt[d, x, p] = value
                py[x, pl.ds(16 * d + p, 8, stride=2), :] = value
        return carry

    lax.fori_loop(0, DUALS, interpolate, 0)

    lane_full = lax.broadcasted_iota(jnp.int32, (128, 128), 1)
    middle = (lane_full >= 32) & (lane_full < 96)

    def to_rows(src, dst):
        for x in range(0, 8, 2):
            both = jnp.where(
                middle, src[x, pl.ds(8, 128), :], pltpu.roll(src[x + 1, pl.ds(8, 128), :], 64, axis=1)
            ).T
            dst[pl.ds(x, 32, stride=16), :] = both[32:64]
            dst[pl.ds(8 + x, 32, stride=16), :] = both[64:96]
            dst[pl.ds(x + 1, 32, stride=16), :] = both[96:128]
            dst[pl.ds(9 + x, 32, stride=16), :] = both[0:32]

    to_rows(py, po)
    low_send = remote(po.at[pl.ds(0, 16)], up_layer, 10, peer(0, 0, -1))
    high_send = remote(po.at[pl.ds(496, 16)], down_pair.at[0], 11, peer(0, 0, 1))
    low_send.start()
    high_send.start()
    press_copy = pltpu.make_async_copy(po, press_out, out_sem.at[0])
    press_copy.start()

    def balance(d, carry):
        val = [[pt[d, x, p] for p in range(2)] for x in range(8)]
        f_e = [[None, None] for _ in range(8)]
        for x in range(8):
            for p in range(2):
                east_v = val[x + 1][p] if x < 7 else lane_roll(val[0][p], -1)
                f_e[x][p] = te[d, x, p] * (val[x][p] - east_v)
        for x in range(8):
            after = sub_roll(jnp.where(row0, pt[d + 1, x, 0], val[x][0]), -1)
            f_n0 = tn[d, x, 0] * (val[x][0] - val[x][1])
            f_n1 = tn[d, x, 1] * (val[x][1] - after)
            before = sub_roll(jnp.where(row7, fp[x], f_n1), 1)
            fp[x] = f_n1
            f_n = (f_n0, f_n1)
            f_s = (before, f_n0)
            for p in range(2):
                f_w = f_e[x - 1][p] if x else lane_roll(f_e[7][p], 1)
                a = at[x, pl.ds(16 * d + p, 8, stride=2), :]
                s = st[x, pl.ds(16 * d + p, 8, stride=2), :]
                flow = a * val[x][p] + (f_e[x][p] - f_w) + (f_n[p] - f_s[p])
                ry[x, pl.ds(16 * d + p, 8, stride=2), :] = s - flow
        return carry

    lax.fori_loop(0, DUALS, balance, 0)
    to_rows(ry, ro)

    def vertical(l, carry):
        r0 = pl.multiple_of(l * 16, 16)
        here = po[pl.ds(r0, 16), :]
        f_up = vt[pl.ds(r0, 16), :] * (here - po[pl.ds(r0 + 16, 16), :])
        ro[pl.ds(r0, 16), :] = ro[pl.ds(r0, 16), :] - f_up + carry
        return f_up

    last_flux = lax.fori_loop(0, LAYERS - 1, vertical, jnp.zeros((16, 128), F32))
    vt_up.wait()
    low_send.wait()
    high_send.wait()
    above = jnp.where(gz < DEPTH - 1, vt[pl.ds(496, 16), :] * (po[pl.ds(496, 16), :] - up_layer[...]), 0.0)
    below = jnp.where(gz > 0, down_pair[1] * (down_pair[0] - po[pl.ds(0, 16), :]), 0.0)
    ro[pl.ds(496, 16), :] = ro[pl.ds(496, 16), :] - above + last_flux
    ro[pl.ds(0, 16), :] = ro[pl.ds(0, 16), :] + below
    resid_copy = pltpu.make_async_copy(ro, resid_out, out_sem.at[1])
    resid_copy.start()
    press_copy.wait()
    resid_copy.wait()


def body(permeability, accumulation, source_term, vertical_trans):
    split = (LAYERS, 2, 8, 128)
    vmem = lambda *shape: pltpu.VMEM(shape, F32)
    anywhere = pl.BlockSpec(memory_space=pl.ANY)
    pressure, residual = pl.pallas_call(
        kernel,
        out_shape=[jax.ShapeDtypeStruct((512, 128), F32)] * 2,
        in_specs=[anywhere] * 4,
        out_specs=[anywhere] * 2,
        scratch_shapes=[
            vmem(4, 32, 8, 128),
            vmem(4, 32, 8, 128),
            vmem(4, 32, 8, 128),
            vmem(512, 128),
            vmem(32, 128),
            vmem(32, 128),
            vmem(9, 152, 128),
            vmem(8, 144, 128),
            vmem(8, 144, 128),
            vmem(9, 8, 2, 8, 128),
            vmem(9, 8, 2, 8, 128),
            vmem(5, 8, 2, 8, 128),
            vmem(3, 9, 8, 2, 8, 128),
            vmem(14, 8, 128),
            vmem(16, 4, 8, 128),
            vmem(2, 24, 128),
            vmem(9, 4, 8, 128),
            vmem(10, 8, 2, 8, 128),
            vmem(8, 144, 128),
            vmem(8, 144, 128),
            vmem(8, 8, 128),
            vmem(512, 128),
            vmem(512, 128),
            vmem(16, 128),
            vmem(2, 16, 128),
            pltpu.SemaphoreType.DMA((7,)),
            pltpu.SemaphoreType.DMA((12,)),
            pltpu.SemaphoreType.DMA((12,)),
            pltpu.SemaphoreType.DMA((16,)),
            pltpu.SemaphoreType.DMA((16,)),
            pltpu.SemaphoreType.DMA((2,)),
        ],
        compiler_params=pltpu.CompilerParams(
            collective_id=0, has_side_effects=True, vmem_limit_bytes=40 * 1024 * 1024
        ),
    )(
        permeability.reshape(split),
        accumulation.reshape(split),
        source_term.reshape(split),
        vertical_trans.reshape(512, 128),
    )
    return pressure.reshape(32, 16, 128), residual.reshape(32, 16, 128)


def solution(mesh):
    spec = P("gz", "gx", "gy")
    return jax.shard_map(
        body, mesh=mesh, in_specs=(spec,) * 4, out_specs=(spec, spec), check_vma=False
    )
```

profile of v0, /device:TPU:1, one launch (start us, length us, event | category | flops | bytes accessed | tf_op | source)
XLA Modules:
  0.0 40.4 jit_solution(14412785275429716335)
XLA Ops:
  0.6 0.0 copy-start
  0.6 0.9 %copy-done = f32[32,16,128]{2,1,0:T(8,128)S(1)} copy-done((f32[32,16,128]{2,1,0:T(8,128)S(1)}, f32[32,16,128]{2,1,0:T(8,128)}, u32[]{:S(2)}) %copy-start) | copy-done | bytes 262168
  1.6 0.0 copy-start.1
  1.6 0.9 %copy-done.1 = f32[32,16,128]{2,1,0:T(8,128)S(1)} copy-done((f32[32,16,128]{2,1,0:T(8,128)S(1)}, f32[32,16,128]{2,1,0:T(8,128)}, u32[]{:S(2)}) %copy-start.1) | copy-done | bytes 262168
  2.5 0.0 copy-start.2
  2.5 0.9 %copy-done.2 = f32[32,16,128]{2,1,0:T(8,128)S(1)} copy-done((f32[32,16,128]{2,1,0:T(8,128)S(1)}, f32[32,16,128]{2,1,0:T(8,128)}, u32[]{:S(2)}) %copy-start.2) | copy-done | bytes 262168
  3.5 0.0 copy-start.3
  3.5 0.9 %copy-done.3 = f32[32,16,128]{2,1,0:T(8,128)S(1)} copy-done((f32[32,16,128]{2,1,0:T(8,128)S(1)}, f32[32,16,128]{2,1,0:T(8,128)}, u32[]{:S(2)}) %copy-start.3) | copy-done | bytes 262168
  4.4 34.5 %shard_map.59 = (f32[512,128]{1,0:T(8,128)S(1)}, f32[512,128]{1,0:T(8,128)S(1)}) custom-call(f32[32,2,8,128]{3,2,1,0:T(8,128)S(1)} %bitcast.8, f32[32,2,8,128]{3,2,1,0:T(8,128)S(1)} %bitcast.9, f32[32,2,8,128]{3,2,1,0:T(8,128)S(1)} %bitcast.10, f32[512,128]{1,0:T(8,128)S(1)} %bitcast.11), custom_call_target="tpu_custom_call" | custom-call | tf_op jit(solution)/shard_map/pallas_call | solution.py:546
  39.0 0.7 %copy.8 = f32[32,16,128]{2,1,0:T(8,128)} copy(f32[32,16,128]{2,1,0:T(8,128)S(1)} %bitcast.7) | data formatting | bytes 524288
  39.7 0.7 %copy.9 = f32[32,16,128]{2,1,0:T(8,128)} copy(f32[32,16,128]{2,1,0:T(8,128)S(1)} %bitcast.6) | data formatting | bytes 524288
Async XLA Ops:
  0.6 1.0 %copy-start = (f32[32,16,128]{2,1,0:T(8,128)S(1)}, f32[32,16,128]{2,1,0:T(8,128)}, u32[]{:S(2)}) copy-start(f32[32,16,128]{2,1,0:T(8,128)} %param.4) | copy-start | bytes 786436
  1.6 0.9 %copy-start.1 = (f32[32,16,128]{2,1,0:T(8,128)S(1)}, f32[32,16,128]{2,1,0:T(8,128)}, u32[]{:S(2)}) copy-start(f32[32,16,128]{2,1,0:T(8,128)} %param.5) | copy-start | bytes 786436
  2.5 0.9 %copy-start.2 = (f32[32,16,128]{2,1,0:T(8,128)S(1)}, f32[32,16,128]{2,1,0:T(8,128)}, u32[]{:S(2)}) copy-start(f32[32,16,128]{2,1,0:T(8,128)} %param.6) | copy-start | bytes 786436
  3.5 0.9 %copy-start.3 = (f32[32,16,128]{2,1,0:T(8,128)S(1)}, f32[32,16,128]{2,1,0:T(8,128)}, u32[]{:S(2)}) copy-start(f32[32,16,128]{2,1,0:T(8,128)} %param.7) | copy-start | bytes 786436
where the time goes:
time: 40.6 us; the launch traced here: 40.4 us
  Pallas kernels  34.5 us (85%)
  local copies, waits for them, and re-layouts  5.2 us (13%)
  between operations  0.65 us (2%)
    pallas_call x1, Pallas kernels, body(): pl.pallas_call(kernel, out_shape=[jax.ShapeDtypeStruct((512, 128), F32)]...  34.5 us
    unnamed x10, local copies, waits for them, and re-layouts  5.2 us

commit v1 on v0

--- a/solution.py
+++ b/solution.py
@@ -219,9 +219,14 @@
         for dy in range(SIDE):
             if dx or dy:
                 pl.semaphore_signal(barrier, inc=1, device_id=peer(dx, dy, 0), device_id_type=MESH)
-    for dz in (-1, 1):
-        pl.semaphore_signal(barrier, inc=1, device_id=peer(0, 0, dz), device_id_type=MESH)
-    pl.semaphore_wait(barrier, 17)
+    has_below, has_above = gz > 0, gz < DEPTH - 1
+    for dz, there in ((-1, has_below), (1, has_above)):
+
+        @pl.when(there)
+        def _():
+            pl.semaphore_signal(barrier, inc=1, device_id=peer(0, 0, dz), device_id_type=MESH)
+
+    pl.semaphore_wait(barrier, 15 + jnp.minimum(gz, 1) + jnp.minimum(DEPTH - 1 - gz, 1))
 
     def remote(src, dst, at_sem, target):
         return pltpu.make_async_remote_copy(
@@ -250,7 +255,10 @@
     for copy in local[2:]:
         copy.wait()
     vt_up = remote(vt.at[pl.ds(496, 16)], down_pair.at[1], 5, peer(0, 0, 1))
-    vt_up.start()
+
+    @pl.when(has_above)
+    def _():
+        vt_up.start()
 
     row = lax.broadcasted_iota(jnp.int32, (8, 128), 0)
     lane = lax.broadcasted_iota(jnp.int32, (8, 128), 1)
@@ -487,8 +495,15 @@
     to_rows(py, po)
     low_send = remote(po.at[pl.ds(0, 16)], up_layer, 10, peer(0, 0, -1))
     high_send = remote(po.at[pl.ds(496, 16)], down_pair.at[0], 11, peer(0, 0, 1))
-    low_send.start()
-    high_send.start()
+
+    @pl.when(has_below)
+    def _():
+        low_send.start()
+
+    @pl.when(has_above)
+    def _():
+        high_send.start()
+
     press_copy = pltpu.make_async_copy(po, press_out, out_sem.at[0])
     press_copy.start()
 
@@ -526,9 +541,19 @@
         return f_up
 
     last_flux = lax.fori_loop(0, LAYERS - 1, vertical, jnp.zeros((16, 128), F32))
-    vt_up.wait()
-    low_send.wait()
-    high_send.wait()
+
+    @pl.when(has_below)
+    def _():
+        vt_up.wait_recv()
+        high_send.wait_recv()
+        low_send.wait_send()
+
+    @pl.when(has_above)
+    def _():
+        low_send.wait_recv()
+        high_send.wait_send()
+        vt_up.wait_send()
+
     above = jnp.where(gz < DEPTH - 1, vt[pl.ds(496, 16), :] * (po[pl.ds(496, 16), :] - up_layer[...]), 0.0)
     below = jnp.where(gz > 0, down_pair[1] * (down_pair[0] - po[pl.ds(0, 16), :]), 0.0)
     ro[pl.ds(496, 16), :] = ro[pl.ds(496, 16), :] - above + last_flux
@@ -543,10 +568,11 @@
     split = (LAYERS, 2, 8, 128)
     vmem = lambda *shape: pltpu.VMEM(shape, F32)
     anywhere = pl.BlockSpec(memory_space=pl.ANY)
+    in_hbm = pl.BlockSpec(memory_space=pltpu.HBM)
     pressure, residual = pl.pallas_call(
         kernel,
         out_shape=[jax.ShapeDtypeStruct((512, 128), F32)] * 2,
-        in_specs=[anywhere] * 4,
+        in_specs=[in_hbm] * 4,
         out_specs=[anywhere] * 2,
         scratch_shapes=[
             vmem(4, 32, 8, 128),
@@ -585,10 +611,15 @@
             collective_id=0, has_side_effects=True, vmem_limit_bytes=40 * 1024 * 1024
         ),
     )(
-        permeability.reshape(split),
-        accumulation.reshape(split),
-        source_term.reshape(split),
-        vertical_trans.reshape(512, 128),
+        *(
+            pltpu.with_memory_space_constraint(value, pltpu.HBM)
+            for value in (
+                permeability.reshape(split),
+                accumulation.reshape(split),
+                source_term.reshape(split),
+                vertical_trans.reshape(512, 128),
+            )
+        ),
     )
     return pressure.reshape(32, 16, 128), residual.reshape(32, 16, 128)
 

time: 40.6 us -> 34.3 us (0.84)
  the two profiles are of different devices: /device:TPU:1 before, /device:TPU:24 now
where the time goes in v1:
time: 34.3 us; the launch traced here: 34.2 us
  Pallas kernels  32.1 us (94%)
  local copies, waits for them, and re-layouts  1.41 us (4%)
  between operations  0.64 us (2%)
    pallas_call x1, Pallas kernels, body(): pl.pallas_call(kernel, out_shape=[jax.ShapeDtypeStruct((512, 128), F32)]...  32.1 us
    unnamed x2, local copies, waits for them, and re-layouts  1.41 us

profile of v1, /device:TPU:24, one launch (start us, length us, event | category | flops | bytes accessed | tf_op | source)
XLA Modules:
  0.0 34.2 jit_solution(8833450835382988169)
XLA Ops:
  0.6 32.1 %shard_map.59 = (f32[512,128]{1,0:T(8,128)S(1)}, f32[512,128]{1,0:T(8,128)S(1)}) custom-call(f32[32,2,8,128]{3,2,1,0:T(8,128)} %bitcast.8, f32[32,2,8,128]{3,2,1,0:T(8,128)} %bitcast.9, f32[32,2,8,128]{3,2,1,0:T(8,128)} %bitcast.10, f32[512,128]{1,0:T(8,128)} %bitcast.11), custom_call_target="tpu_custom_call" | custom-call | tf_op jit(solution)/shard_map/pallas_call | solution.py:572
  32.8 0.7 %copy.8 = f32[32,16,128]{2,1,0:T(8,128)} copy(f32[32,16,128]{2,1,0:T(8,128)S(1)} %bitcast.7) | data formatting | bytes 524288
  33.5 0.7 %copy.9 = f32[32,16,128]{2,1,0:T(8,128)} copy(f32[32,16,128]{2,1,0:T(8,128)S(1)} %bitcast.6) | data formatting | bytes 524288

commit v2 on v1

--- a/solution.py
+++ b/solution.py
@@ -12,7 +12,7 @@
 DUALS = 9
 MESH = pl.DeviceIdType.MESH
 F32 = jnp.float32
-LX, LY, LXY = 0, 1, 2
+LX, LY = 0, 1
 
 
 def lane_roll(value, groups):
@@ -189,7 +189,8 @@
 
 def kernel(
     perm, accum, source, vtrans, press_out, resid_out,
-    hx, ax, sx, vt, row24, row8, tp, at, st, te, tn, co, bf, sums, ga, nodes, cb, pt, py, ry, fp, po, ro,
+    hx, ax, sx, vt, row24, row8, lo_out, hi_out, lo_n, lo_ne0, lo_ne1, lo_nw, hi_s, hi_se0, hi_se1, hi_sw,
+    tp, ta, ts, teq, tnq, bq, tew, tnw, bw, te, tn, bf, co, sums, ga, gk, nodes, cb, pt, py, ry, fp, po, ro,
     up_layer, down_pair,
     local_sem, send_sem, recv_sem, gsend_sem, grecv_sem, out_sem,
 ):
@@ -205,26 +206,58 @@
     local = [
         pltpu.make_async_copy(perm.at[:, 0], hx.at[1], local_sem.at[0]),
         pltpu.make_async_copy(perm.at[:, 1], hx.at[2], local_sem.at[1]),
-        pltpu.make_async_copy(accum.at[:, 0], ax.at[1], local_sem.at[2]),
-        pltpu.make_async_copy(accum.at[:, 1], ax.at[2], local_sem.at[3]),
-        pltpu.make_async_copy(source.at[:, 0], sx.at[1], local_sem.at[4]),
-        pltpu.make_async_copy(source.at[:, 1], sx.at[2], local_sem.at[5]),
+        pltpu.make_async_copy(accum.at[:, 0], ax.at[0], local_sem.at[2]),
+        pltpu.make_async_copy(accum.at[:, 1], ax.at[1], local_sem.at[3]),
+        pltpu.make_async_copy(source.at[:, 0], sx.at[0], local_sem.at[4]),
+        pltpu.make_async_copy(source.at[:, 1], sx.at[1], local_sem.at[5]),
         pltpu.make_async_copy(vtrans, vt, local_sem.at[6]),
     ]
     for copy in local:
         copy.start()
 
+    has_below, has_above = gz > 0, gz < DEPTH - 1
     barrier = pltpu.get_barrier_semaphore()
     for dx in range(SIDE):
         for dy in range(SIDE):
             if dx or dy:
                 pl.semaphore_signal(barrier, inc=1, device_id=peer(dx, dy, 0), device_id_type=MESH)
-    has_below, has_above = gz > 0, gz < DEPTH - 1
     for dz, there in ((-1, has_below), (1, has_above)):
 
         @pl.when(there)
         def _():
             pl.semaphore_signal(barrier, inc=1, device_id=peer(0, 0, dz), device_id_type=MESH)
+
+    row = lax.broadcasted_iota(jnp.int32, (8, 128), 0)
+    lane = lax.broadcasted_iota(jnp.int32, (8, 128), 1)
+    group = lane // 32
+    lower = lane < 64
+    u_base = jnp.where(group % 2 == 1, 8, 0)
+    row0 = row == 0
+    row7 = row == 7
+    u0 = u_base == 0
+    u8 = u_base == 8
+
+    hx_rows = hx.reshape(4 * 256, 128)
+    ax_rows = ax.reshape(3 * 256, 128)
+    sx_rows = sx.reshape(3 * 256, 128)
+
+    def edges(rows, base, at_row, depth, with_high):
+        for half in range(2):
+            for m in range(2):
+                first = base + 256 * half + 4 * m
+                turned = jnp.concatenate([rows[pl.ds(first + q, 32, stride=8), :] for q in range(4)], axis=0).T
+                lo_out[half, m, pl.ds(at_row, depth), :] = turned[:depth]
+                if with_high:
+                    hi_out[half, m] = turned[120:]
+
+    local[0].wait()
+    local[1].wait()
+    row8[...] = hx_rows[pl.ds(512, LAYERS, stride=8), :]
+    edges(hx_rows, 256, 0, 16, True)
+    for copy in local[2:]:
+        copy.wait()
+    edges(ax_rows, 0, 16, 8, False)
+    edges(sx_rows, 0, 24, 8, False)
 
     pl.semaphore_wait(barrier, 15 + jnp.minimum(gz, 1) + jnp.minimum(DEPTH - 1 - gz, 1))
 
@@ -236,129 +269,161 @@
 
     west, east = peer(-1, 0, 0), peer(1, 0, 0)
     south, north = peer(0, -1, 0), peer(0, 1, 0)
-    perm_w = remote(perm.at[:, 0], hx.at[3], 0, west)
-    perm_e = remote(perm.at[:, 1], hx.at[0], 1, east)
-    perm_w.start()
-    perm_e.start()
-    for copy in local[:2]:
-        copy.wait()
-    hx_rows = hx.reshape(4 * 256, 128)
-    ax_rows = ax.reshape(4 * 256, 128)
-    sx_rows = sx.reshape(4 * 256, 128)
-    row8[...] = hx_rows[pl.ds(512, LAYERS, stride=8), :]
-    perm_r = remote(row8, row24, 2, west)
-    perm_r.start()
-    accum_w = remote(accum.at[:, 0], ax.at[3], 3, west)
-    source_w = remote(source.at[:, 0], sx.at[3], 4, west)
-    accum_w.start()
-    source_w.start()
-    for copy in local[2:]:
-        copy.wait()
-    vt_up = remote(vt.at[pl.ds(496, 16)], down_pair.at[1], 5, peer(0, 0, 1))
+    perm_w = remote(hx.at[1], hx.at[3], 0, west)
+    perm_r = remote(row8, row24, 1, west)
+    low_s = remote(lo_out, lo_n, 2, south)
+    low_sw0 = remote(lo_out.at[0], lo_ne0, 3, peer(-1, -1, 0))
+    low_sw1 = remote(lo_out.at[1, 0, pl.ds(0, 16)], lo_ne1, 4, peer(-1, -1, 0))
+    accum_w = remote(ax.at[0], ax.at[2], 5, west)
+    source_w = remote(sx.at[0], sx.at[2], 6, west)
+    perm_e = remote(hx.at[2], hx.at[0], 7, east)
+    low_se = remote(lo_out.at[1, :, pl.ds(0, 16)], lo_nw, 8, peer(1, -1, 0))
+    high_n = remote(hi_out, hi_s, 9, north)
+    high_nw0 = remote(hi_out.at[0], hi_se0, 10, peer(-1, 1, 0))
+    high_nw1 = remote(hi_out.at[1, 0], hi_se1, 11, peer(-1, 1, 0))
+    high_ne = remote(hi_out.at[1], hi_sw, 12, peer(1, 1, 0))
+    vt_up = remote(vt.at[pl.ds(496, 16)], down_pair.at[1], 13, peer(0, 0, 1))
+    first_sends = [perm_w, perm_r, low_s, low_sw0, low_sw1, accum_w, source_w]
+    later_sends = [perm_e, low_se, high_n, high_nw0, high_nw1, high_ne]
+    for copy in first_sends + later_sends:
+        copy.start()
 
     @pl.when(has_above)
     def _():
         vt_up.start()
 
-    row = lax.broadcasted_iota(jnp.int32, (8, 128), 0)
-    lane = lax.broadcasted_iota(jnp.int32, (8, 128), 1)
-    group = lane // 32
-    u_base = jnp.where(group % 2 == 1, 8, 0)
-    row0 = row == 0
-    row7 = row == 7
-    u0 = u_base == 0
-    u8 = u_base == 8
-
-    perm_w.wait()
-    perm_e.wait()
-    perm_r.wait()
-    for x in range(8):
-        tp[x, pl.ds(8, 128), :] = hx_rows[pl.ds(x, 128, stride=8), :].T
-    tp[8, pl.ds(8, 128), :] = jnp.concatenate(
-        [hx_rows[pl.ds(256, 96, stride=8), :], row24[...]], axis=0
-    ).T
-    strip_s = remote(tp.at[:, pl.ds(8, 16), :], tp.at[:, pl.ds(136, 16), :], 6, south)
-    strip_n = remote(tp.at[:, pl.ds(128, 8), :], tp.at[:, pl.ds(0, 8), :], 7, north)
-    strip_s.start()
-    strip_n.start()
-    accum_s = remote(at.at[:, pl.ds(8, 8), :], at.at[:, pl.ds(136, 8), :], 8, south)
-    source_s = remote(st.at[:, pl.ds(8, 8), :], st.at[:, pl.ds(136, 8), :], 9, south)
-
-    def relax(k, carry):
-        d = lax.rem(k + 1, DUALS)
-
-        @pl.when(k == 3)
-        def _():
-            accum_w.wait()
-            source_w.wait()
+    def pick(at_group, left, by_left, right, by_right):
+        return jnp.where(group == at_group, lane_roll(left, by_left), lane_roll(right, by_right))
+
+    perm_w.wait_recv()
+    perm_r.wait_recv()
+    for x in range(9):
+        if x < 8:
+            part = hx_rows[pl.ds(512 + x, 64, stride=8), :]
+        else:
+            part = jnp.concatenate([hx_rows[pl.ds(768, 32, stride=8), :], row24[...]], axis=0)
+        tp[1, x, pl.ds(8, 128), :] = jnp.concatenate([part, part], axis=0).T
+
+    def north_owned():
+        low_s.wait_recv()
+        low_sw0.wait_recv()
+        low_sw1.wait_recv()
+        for t in range(2):
+            at = pl.ds(8 * t, 8)
             for x in range(8):
-                at[x, pl.ds(8, 128), :] = ax_rows[pl.ds(x, 128, stride=8), :].T
-                st[x, pl.ds(8, 128), :] = sx_rows[pl.ds(x, 128, stride=8), :].T
-            accum_s.start()
-            source_s.start()
-
-        @pl.when(k == 7)
-        def _():
-            strip_s.wait()
-            strip_n.wait()
-
-        cells = [[tp[x, pl.ds(16 * d + p, 8, stride=2), :] for p in range(2)] for x in range(9)]
+                m, q = x // 4, x % 4
+                tp[1, x, pl.ds(136 + 8 * t, 8), :] = pick(2, lo_n[1, m, at, :], 2 - q, lo_ne0[m, at, :], 3 - q)
+            tp[1, 8, pl.ds(136 + 8 * t, 8), :] = pick(2, lo_ne0[0, at, :], 2, lo_ne1[at, :], 3)
+
+    def relax(sel_lo, sel_hi, at_lo, at_hi, put_t, put_b):
+        def cell(x, off):
+            return jnp.where(
+                lower,
+                tp[sel_lo, x, pl.ds(at_lo + off, 8, stride=2), :],
+                tp[sel_hi, x, pl.ds(at_hi + off, 8, stride=2), :],
+            )
+
+        cells = [[cell(x, p) for p in range(2)] for x in range(9)]
         t_e = [[harmonic(cells[x][p], cells[x + 1][p]) for p in range(2)] for x in range(8)]
         for x in range(8):
-            after = tp[x, pl.ds(16 * d + 2, 8, stride=2), :]
-            t_n = [harmonic(cells[x][0], cells[x][1]), harmonic(cells[x][1], after)]
+            t_n = [harmonic(cells[x][0], cells[x][1]), harmonic(cells[x][1], cell(x, 2))]
             t_s = [sub_roll(t_n[1], 1), t_n[0]]
             for p in range(2):
                 t_w = t_e[x - 1][p] if x else lane_roll(t_e[7][p], 1)
-                te[d, x, p] = t_e[x][p]
-                tn[d, x, p] = t_n[p]
+                put_t(x, p, t_e[x][p], t_n[p])
                 inv = inverse((t_w + t_e[x][p]) + (t_s[p] + t_n[p]))
+                if p == 0 and x == 0:
+                    inv = jnp.where(row0 | u0, 0.0, inv)
+                elif p == 0:
+                    inv = jnp.where(row0, 0.0, inv)
+                elif x == 0:
+                    inv = jnp.where(u0, 0.0, inv)
                 co[0, x, p] = t_w * inv
                 co[1, x, p] = t_e[x][p] * inv
                 co[2, x, p] = t_s[p] * inv
                 co[3, x, p] = t_n[p] * inv
-            co[4, x, 0] = jnp.where(row7, 0.0, co[3, x, 1])
-        co[4, 0, 1] = jnp.where(u8, 0.0, co[1, 7, 0])
-        co[4, 1, 1] = jnp.where(u8, 0.0, co[1, 7, 1])
-
-        fixed = [[row0 | u0, u0]] + [[row0, None]] * 7
-        for kind in range(3):
-            vals = []
+
+        def sweep(vals):
+            new = []
             for x in range(8):
-                along_x = 1.0 - (u_base + x).astype(F32) / 16.0
                 pair = []
                 for p in range(2):
-                    along_y = 1.0 - (2 * row + p).astype(F32) / 16.0
-                    pair.append((along_x, along_y, along_x * along_y)[kind])
-                vals.append(pair)
-            for _ in range(SWEEPS):
-                new = []
-                for x in range(8):
-                    pair = []
-                    for p in range(2):
-                        west_v = vals[x - 1][p] if x else lane_roll(vals[7][p], 1)
-                        east_v = vals[x + 1][p] if x < 7 else lane_roll(vals[0][p], -1)
-                        south_v = vals[x][0] if p else sub_roll(vals[x][1], 1)
-                        north_v = sub_roll(vals[x][0], -1) if p else vals[x][1]
-                        c_e = co[4, p, 1] if x == 7 and kind != LY else co[1, x, p]
-                        c_n = co[4, x, 0] if p and kind != LX else co[3, x, p]
-                        value = (co[0, x, p] * west_v + c_e * east_v) + (co[2, x, p] * south_v + c_n * north_v)
-                        keep = fixed[x][p]
-                        pair.append(value if keep is None else jnp.where(keep, vals[x][p], value))
-                    new.append(pair)
-                vals = new
+                    west_v = vals[x - 1][p] if x else lane_roll(vals[7][p], 1)
+                    east_v = vals[x + 1][p] if x < 7 else lane_roll(vals[0][p], -1)
+                    south_v = vals[x][0] if p else sub_roll(vals[x][1], 1)
+                    north_v = sub_roll(vals[x][0], -1) if p else vals[x][1]
+                    pair.append(
+                        (co[0, x, p] * west_v + co[1, x, p] * east_v) + (co[2, x, p] * south_v + co[3, x, p] * north_v)
+                    )
+                new.append(pair)
+            return new
+
+        def plus(left, right):
+            return [[left[x][p] + right[x][p] for p in range(2)] for x in range(8)]
+
+        def along(x, p):
+            return 1.0 - (u_base + x).astype(F32) / 16.0, 1.0 - (2 * row + p).astype(F32) / 16.0
+
+        for kind in range(3):
+            push = []
+            for x in range(8):
+                pair = []
+                for p in range(2):
+                    w_x, w_y = along(x, p)
+                    if kind == LX:
+                        value = co[0, x, p] - co[1, x, p]
+                    elif kind == LY:
+                        value = co[2, x, p] - co[3, x, p]
+                    else:
+                        value = (co[0, x, p] - co[1, x, p]) * w_y + (co[2, x, p] - co[3, x, p]) * w_x
+                    pair.append(value)
+                push.append(pair)
+            vals = plus(push, sweep(push))
+            vals = plus(vals, sweep(sweep(vals)))
+            vals = plus(vals, sweep(sweep(sweep(sweep(vals)))))
             for x in range(8):
                 for p in range(2):
-                    bf[kind, d, x, p] = vals[x][p]
+                    w_x, w_y = along(x, p)
+                    put_b(kind, x, p, (w_x, w_y, w_x * w_y)[kind] + vals[x][p] * (1.0 / 16.0))
+
+    def owned(k, carry):
+        @pl.when(k == 3)
+        def _():
+            north_owned()
+
+        at_lo = 16 + 16 * lax.rem(k, 2) + 64 * (k // 2)
+
+        def put_t(x, p, east_t, north_t):
+            teq[k, x, p] = east_t
+            tnq[k, x, p] = north_t
+
+        def put_b(kind, x, p, value):
+            bq[kind, k, x, p] = value
+
+        relax(1, 1, at_lo, at_lo + 32, put_t, put_b)
         return carry
 
-    lax.fori_loop(0, DUALS, relax, 0)
-
-    def gram(d, carry):
-        @pl.when(d == 8)
-        def _():
-            accum_s.wait()
-            source_s.wait()
+    lax.fori_loop(0, 4, owned, 0)
+
+    accum_w.wait_recv()
+    source_w.wait_recv()
+    for rows, turned, at_row in ((ax_rows, ta, 16), (sx_rows, ts, 24)):
+        for x in range(8):
+            m, q = x // 4, x % 4
+            part = rows[pl.ds(256 + x, 64, stride=8), :]
+            turned[x, pl.ds(0, 128), :] = jnp.concatenate([part, part], axis=0).T
+            at = pl.ds(at_row, 8)
+            turned[x, pl.ds(128, 8), :] = pick(2, lo_n[1, m, at, :], 2 - q, lo_ne0[m, at, :], 3 - q)
+
+    def gram(k, carry):
+        at_lo = 8 + 16 * lax.rem(k, 2) + 64 * (k // 2)
+
+        def load(ref, x, p):
+            return jnp.where(
+                lower,
+                ref[x, pl.ds(at_lo + p, 8, stride=2), :],
+                ref[x, pl.ds(at_lo + 32 + p, 8, stride=2), :],
+            )
 
         acc = {}
 
@@ -367,24 +432,24 @@
 
         for x in range(8):
             for p in range(2):
-                a = at[x, pl.ds(16 * d + p, 8, stride=2), :]
-                s = st[x, pl.ds(16 * d + p, 8, stride=2), :]
-                here = [bf[kind, d, x, p] for kind in range(3)]
-                t_e, t_n = te[d, x, p], tn[d, x, p]
+                a = load(ta, x, p)
+                s = load(ts, x, p)
+                here = [bq[kind, k, x, p] for kind in range(3)]
+                t_e, t_n = teq[k, x, p], tnq[k, x, p]
                 mass, d_e, d_n = [], [], []
                 for kind in range(3):
                     if x < 7:
-                        east_v = bf[kind, d, x + 1, p]
+                        east_v = bq[kind, k, x + 1, p]
                     else:
-                        east_v = lane_roll(bf[kind, d, 0, p], -1)
+                        east_v = lane_roll(bq[kind, k, 0, p], -1)
                         if kind != LY:
                             east_v = jnp.where(u8, 0.0, east_v)
                     if p:
-                        north_v = sub_roll(bf[kind, d, x, 0], -1)
+                        north_v = sub_roll(bq[kind, k, x, 0], -1)
                         if kind != LX:
                             north_v = jnp.where(row7, 0.0, north_v)
                     else:
-                        north_v = bf[kind, d, x, 1]
+                        north_v = bq[kind, k, x, 1]
                     d_e.append(here[kind] - east_v)
                     d_n.append(here[kind] - north_v)
                     mass.append(a * here[kind])
@@ -396,53 +461,133 @@
                     w_e, w_n = t_e * d_e[kind], t_n * d_n[kind]
                     for other in range(kind, 3):
                         add((kind + 1, other + 1), mass[kind] * here[other] + w_e * d_e[other] + w_n * d_n[other])
-        mine = row == d - 1
         for index, key in enumerate(GRAM + ("r0", "r1", "r2", "r3")):
             value = acc[key]
             value = value + sub_roll(value, 4)
             value = value + sub_roll(value, 2)
             value = value + sub_roll(value, 1)
-            sums[index] = jnp.where(mine, value, sums[index])
+            sums[k, index] = value + lane_roll(value, -1)
         return carry
 
-    lax.fori_loop(1, DUALS, gram, 0)
-
-    whole = []
-    for index in range(14):
-        value = sums[index]
-        whole.append(value + lane_roll(value, -1))
-    entries = corner_sums({key: whole[i] for i, key in enumerate(GRAM)}, whole[10:])
-    for k in range(4):
-        packed = jnp.zeros((8, 128), F32)
-        for q in range(4):
-            if 4 * k + q < 14:
-                packed = jnp.where(group == q, lane_roll(entries[4 * k + q], q - 2), packed)
-        ga[0, k] = packed
-    gathers = []
-    for dx in range(SIDE):
-        for dy in range(SIDE):
-            if dx or dy:
-                slot = (-dx % SIDE) * SIDE + (-dy % SIDE)
-                gathers.append(
-                    pltpu.make_async_remote_copy(
-                        src_ref=ga.at[0], dst_ref=ga.at[slot],
-                        send_sem=gsend_sem.at[slot], recv_sem=grecv_sem.at[slot],
-                        device_id=peer(dx, dy, 0), device_id_type=MESH,
+    def send_sums(piece):
+        whole = []
+        for index in range(14):
+            value = jnp.where(row % 2 == 1, sums[2 * piece + 1, index], sums[2 * piece, index])
+            whole.append(jnp.where(row % 4 < 2, value, lane_roll(value, -2)))
+        entries = corner_sums({key: whole[i] for i, key in enumerate(GRAM)}, whole[10:])
+        for m in range(2):
+            packed = jnp.zeros((8, 128), F32)
+            for t in range(8 * m, min(8 * m + 8, 14)):
+                here = (group == t % 4) & (row // 4 == t // 4 % 2)
+                packed = jnp.where(here, lane_roll(entries[t], t % 4), packed)
+            ga[piece, 0, m] = packed
+        copies = []
+        for dx in range(SIDE):
+            for dy in range(SIDE):
+                if dx or dy:
+                    slot = (-dx % SIDE) * SIDE + (-dy % SIDE)
+                    copies.append(
+                        pltpu.make_async_remote_copy(
+                            src_ref=ga.at[piece, 0], dst_ref=ga.at[piece, slot],
+                            send_sem=gsend_sem.at[piece, slot], recv_sem=grecv_sem.at[piece, slot],
+                            device_id=peer(dx, dy, 0), device_id_type=MESH,
+                        )
                     )
-                )
-    for copy in gathers:
-        copy.start()
+        for copy in copies:
+            copy.start()
+        return copies
+
+    lax.fori_loop(0, 2, gram, 0)
+    gathers = send_sums(0)
+    lax.fori_loop(2, 4, gram, 0)
+    gathers = gathers + send_sums(1)
+
+    for copy in later_sends:
+        copy.wait_recv()
+    for x in range(9):
+        part = hx_rows[pl.ds(x if x < 8 else 256, 64, stride=8), :]
+        tp[0, x, pl.ds(8, 128), :] = jnp.concatenate([part, part], axis=0).T
+    for x in range(8):
+        m, q = x // 4, x % 4
+        for t in range(2):
+            at = pl.ds(8 * t, 8)
+            tp[0, x, pl.ds(136 + 8 * t, 8), :] = pick(2, lo_nw[m, at, :], 2 - q, lo_n[0, m, at, :], 3 - q)
+        tp[0, x, pl.ds(0, 8), :] = pick(0, hi_sw[m], -q, hi_s[0, m], 1 - q)
+        tp[1, x, pl.ds(0, 8), :] = pick(2, hi_s[1, m], 2 - q, hi_se0[m], 3 - q)
+    for t in range(2):
+        at = pl.ds(8 * t, 8)
+        tp[0, 8, pl.ds(136 + 8 * t, 8), :] = pick(2, lo_n[0, 0, at, :], 2, lo_n[1, 0, at, :], 3)
+    tp[0, 8, pl.ds(0, 8), :] = pick(0, hi_s[0, 0], 0, hi_s[1, 0], 1)
+    tp[1, 8, pl.ds(0, 8), :] = pick(2, hi_se0[0], 2, hi_se1[...], 3)
+
+    def others(k, carry):
+        edge = k // 4
+        at_lo = (16 + 16 * lax.rem(k, 2) + 64 * (k // 2)) * (1 - edge)
+
+        def put_t(x, p, east_t, north_t):
+            tew[x, p] = east_t
+            tnw[x, p] = north_t
+
+        def put_b(kind, x, p, value):
+            bw[kind, x, p] = value
+
+        relax(0, edge, at_lo, at_lo + 32 * (1 - edge), put_t, put_b)
+
+        @pl.when(k < 4)
+        def _():
+            d_lo = 1 + lax.rem(k, 2) + 4 * (k // 2)
+
+            def merge(own, other, put):
+                crossed = pltpu.roll(jnp.where(lower, own, other), 64, axis=1)
+                put(d_lo, jnp.where(lower, other, crossed))
+                put(d_lo + 2, jnp.where(lower, crossed, own))
+
+            for x in range(8):
+                for p in range(2):
+
+                    def put_te(d, value):
+                        te[d, x, p] = value
+
+                    def put_tn(d, value):
+                        tn[d, x, p] = value
+
+                    merge(teq[k, x, p], tew[x, p], put_te)
+                    merge(tnq[k, x, p], tnw[x, p], put_tn)
+                    for kind in range(3):
+
+                        def put_bf(d, value):
+                            bf[kind, d, x, p] = value
+
+                        merge(bq[kind, k, x, p], bw[kind, x, p], put_bf)
+
+        @pl.when(k == 4)
+        def _():
+            te[0] = tew[...]
+            tn[0] = tnw[...]
+            for kind in range(3):
+                bf[kind, 0] = bw[kind]
+
+        return carry
+
+    lax.fori_loop(0, 5, others, 0)
+
     for copy in gathers:
         copy.wait()
+    for slot in range(SIDE * SIDE):
+        for m in range(2):
+            first, second = ga[0, slot, m], ga[1, slot, m]
+            crossed = sub_roll(jnp.where(row < 4, second, first), 4)
+            gk[slot, 2 * m] = jnp.where(row < 4, first, crossed)
+            gk[slot, 2 * m + 1] = jnp.where(row < 4, crossed, second)
 
     table = []
     for index in range(14):
         k, q = index // 4, index % 4
         by_x = []
         for i in range(SIDE):
-            value = lane_roll(ga[i * SIDE, k], -q)
+            value = lane_roll(gk[i * SIDE, k], -q)
             for g in range(1, SIDE):
-                value = jnp.where(group == g, lane_roll(ga[i * SIDE + g, k], g - q), value)
+                value = jnp.where(group == g, lane_roll(gk[i * SIDE + g, k], g - q), value)
             by_x.append(value)
         table.append(by_x)
     b, c, d_side = assemble(table, row)
@@ -453,11 +598,10 @@
         value = value + lane_roll(value, 1)
         return value + lane_roll(value, 2)
 
-    first_half = lane < 64
     for at_row, g in ((0, 3), (8, 0), (16, 1)):
         mid = everywhere(coarse[0], g)
-        nodes[0, pl.ds(at_row, 8), :] = jnp.where(first_half, everywhere(coarse[3], g), mid)
-        nodes[1, pl.ds(at_row, 8), :] = jnp.where(first_half, mid, everywhere(coarse[1], g))
+        nodes[0, pl.ds(at_row, 8), :] = jnp.where(lower, everywhere(coarse[3], g), mid)
+        nodes[1, pl.ds(at_row, 8), :] = jnp.where(lower, mid, everywhere(coarse[1], g))
     for d in range(DUALS):
         c0 = jnp.broadcast_to(nodes[0, pl.ds(7 + d, 1), :], (8, 128))
         c1 = jnp.broadcast_to(nodes[1, pl.ds(7 + d, 1), :], (8, 128))
@@ -493,8 +637,8 @@
             dst[pl.ds(9 + x, 32, stride=16), :] = both[0:32]
 
     to_rows(py, po)
-    low_send = remote(po.at[pl.ds(0, 16)], up_layer, 10, peer(0, 0, -1))
-    high_send = remote(po.at[pl.ds(496, 16)], down_pair.at[0], 11, peer(0, 0, 1))
+    low_send = remote(po.at[pl.ds(0, 16)], up_layer, 14, peer(0, 0, -1))
+    high_send = remote(po.at[pl.ds(496, 16)], down_pair.at[0], 15, peer(0, 0, 1))
 
     @pl.when(has_below)
     def _():
@@ -524,23 +668,24 @@
             f_s = (before, f_n0)
             for p in range(2):
                 f_w = f_e[x - 1][p] if x else lane_roll(f_e[7][p], 1)
-                a = at[x, pl.ds(16 * d + p, 8, stride=2), :]
-                s = st[x, pl.ds(16 * d + p, 8, stride=2), :]
-                flow = a * val[x][p] + (f_e[x][p] - f_w) + (f_n[p] - f_s[p])
-                ry[x, pl.ds(16 * d + p, 8, stride=2), :] = s - flow
+                ry[x, pl.ds(16 * d + p, 8, stride=2), :] = (f_e[x][p] - f_w) + (f_n[p] - f_s[p])
         return carry
 
     lax.fori_loop(0, DUALS, balance, 0)
     to_rows(ry, ro)
 
-    def vertical(l, carry):
-        r0 = pl.multiple_of(l * 16, 16)
-        here = po[pl.ds(r0, 16), :]
-        f_up = vt[pl.ds(r0, 16), :] * (here - po[pl.ds(r0 + 16, 16), :])
-        ro[pl.ds(r0, 16), :] = ro[pl.ds(r0, 16), :] - f_up + carry
-        return f_up
-
-    last_flux = lax.fori_loop(0, LAYERS - 1, vertical, jnp.zeros((16, 128), F32))
+    for half in range(2):
+        before = None
+        for l in range(LAYERS):
+            at = pl.ds(16 * l + 8 * half, 8)
+            here = po[at, :]
+            value = sx[half, l] - ax[half, l] * here - ro[at, :]
+            if before is not None:
+                value = value + before
+            if l < LAYERS - 1:
+                before = vt[at, :] * (here - po[pl.ds(16 * (l + 1) + 8 * half, 8), :])
+                value = value - before
+            ro[at, :] = value
 
     @pl.when(has_below)
     def _():
@@ -554,12 +699,14 @@
         high_send.wait_send()
         vt_up.wait_send()
 
-    above = jnp.where(gz < DEPTH - 1, vt[pl.ds(496, 16), :] * (po[pl.ds(496, 16), :] - up_layer[...]), 0.0)
-    below = jnp.where(gz > 0, down_pair[1] * (down_pair[0] - po[pl.ds(0, 16), :]), 0.0)
-    ro[pl.ds(496, 16), :] = ro[pl.ds(496, 16), :] - above + last_flux
+    above = jnp.where(has_above, vt[pl.ds(496, 16), :] * (po[pl.ds(496, 16), :] - up_layer[...]), 0.0)
+    below = jnp.where(has_below, down_pair[1] * (down_pair[0] - po[pl.ds(0, 16), :]), 0.0)
+    ro[pl.ds(496, 16), :] = ro[pl.ds(496, 16), :] - above
     ro[pl.ds(0, 16), :] = ro[pl.ds(0, 16), :] + below
     resid_copy = pltpu.make_async_copy(ro, resid_out, out_sem.at[1])
     resid_copy.start()
+    for copy in first_sends + later_sends:
+        copy.wait_send()
     press_copy.wait()
     resid_copy.wait()
 
@@ -576,19 +723,36 @@
         out_specs=[anywhere] * 2,
         scratch_shapes=[
             vmem(4, 32, 8, 128),
-            vmem(4, 32, 8, 128),
-            vmem(4, 32, 8, 128),
+            vmem(3, 32, 8, 128),
+            vmem(3, 32, 8, 128),
             vmem(512, 128),
             vmem(32, 128),
             vmem(32, 128),
-            vmem(9, 152, 128),
-            vmem(8, 144, 128),
-            vmem(8, 144, 128),
+            vmem(2, 2, 32, 128),
+            vmem(2, 2, 8, 128),
+            vmem(2, 2, 32, 128),
+            vmem(2, 32, 128),
+            vmem(16, 128),
+            vmem(2, 16, 128),
+            vmem(2, 2, 8, 128),
+            vmem(2, 8, 128),
+            vmem(8, 128),
+            vmem(2, 8, 128),
+            vmem(2, 9, 152, 128),
+            vmem(8, 136, 128),
+            vmem(8, 136, 128),
+            vmem(4, 8, 2, 8, 128),
+            vmem(4, 8, 2, 8, 128),
+            vmem(3, 4, 8, 2, 8, 128),
+            vmem(8, 2, 8, 128),
+            vmem(8, 2, 8, 128),
+            vmem(3, 8, 2, 8, 128),
             vmem(9, 8, 2, 8, 128),
             vmem(9, 8, 2, 8, 128),
-            vmem(5, 8, 2, 8, 128),
             vmem(3, 9, 8, 2, 8, 128),
-            vmem(14, 8, 128),
+            vmem(4, 8, 2, 8, 128),
+            vmem(4, 14, 8, 128),
+            vmem(2, 16, 2, 8, 128),
             vmem(16, 4, 8, 128),
             vmem(2, 24, 128),
             vmem(9, 4, 8, 128),
@@ -601,10 +765,10 @@
             vmem(16, 128),
             vmem(2, 16, 128),
             pltpu.SemaphoreType.DMA((7,)),
-            pltpu.SemaphoreType.DMA((12,)),
-            pltpu.SemaphoreType.DMA((12,)),
             pltpu.SemaphoreType.DMA((16,)),
             pltpu.SemaphoreType.DMA((16,)),
+            pltpu.SemaphoreType.DMA((2, 16)),
+            pltpu.SemaphoreType.DMA((2, 16)),
             pltpu.SemaphoreType.DMA((2,)),
         ],
         compiler_params=pltpu.CompilerParams(

time: 34.3 us -> 31.2 us (0.910)
  the two profiles are of different devices: /device:TPU:24 before, /device:TPU:25 now
where the time goes in v2:
time: 31.2 us; the launch traced here: 31.1 us
  Pallas kernels  29.1 us (93%)
  local copies, waits for them, and re-layouts  1.41 us (5%)
  between operations  0.64 us (2%)
    pallas_call x1, Pallas kernels, body(): pl.pallas_call(kernel, out_shape=[jax.ShapeDtypeStruct((512, 128), F32)]...  29.1 us
    unnamed x2, local copies, waits for them, and re-layouts  1.41 us

profile of v2, /device:TPU:25, one launch (start us, length us, event | category | flops | bytes accessed | tf_op | source)
XLA Modules:
  0.0 31.1 jit_solution(4249016868922336024)
XLA Ops:
  0.6 29.1 %shard_map.59 = (f32[512,128]{1,0:T(8,128)S(1)}, f32[512,128]{1,0:T(8,128)S(1)}) custom-call(f32[32,2,8,128]{3,2,1,0:T(8,128)} %bitcast.8, f32[32,2,8,128]{3,2,1,0:T(8,128)} %bitcast.9, f32[32,2,8,128]{3,2,1,0:T(8,128)} %bitcast.10, f32[512,128]{1,0:T(8,128)} %bitcast.11), custom_call_target="tpu_custom_call" | custom-call | tf_op jit(solution)/shard_map/pallas_call | solution.py:719
  29.7 0.7 %copy.8 = f32[32,16,128]{2,1,0:T(8,128)} copy(f32[32,16,128]{2,1,0:T(8,128)S(1)} %bitcast.7) | data formatting | bytes 524288
  30.4 0.7 %copy.9 = f32[32,16,128]{2,1,0:T(8,128)} copy(f32[32,16,128]{2,1,0:T(8,128)S(1)} %bitcast.6) | data formatting | bytes 524288

commit v3 on v2

v3 whole, which is shorter than its diff:
```python
import jax
import jax.numpy as jnp
from jax import lax
from jax.experimental import pallas as pl
from jax.experimental.pallas import tpu as pltpu
from jax.sharding import PartitionSpec as P

LAYERS = 32
SETS = 2
SIDE = 4
DEPTH = 16
MIDDLE = DEPTH // 2
DUALS = 9
MESH = pl.DeviceIdType.MESH
F32 = jnp.float32
LX, LY = 0, 1


def lane_roll(value, groups):
    by = (groups * 16) % 128
    return value if by == 0 else pltpu.roll(value, by, axis=1)


def sub_roll(value, by):
    return pltpu.roll(value, by % 8, axis=0)


def inverse(value, rounds=1):
    guess = pl.reciprocal(value, approx=True)
    for _ in range(rounds):
        guess = guess * (2.0 - value * guess)
    return guess


def harmonic(left, right):
    return 2.0 * left * right * inverse(left + right)


def node_shift(value, by, slot):
    if by % 4 == 0:
        return sub_roll(value, -(by // 4))
    turned = lane_roll(value, -2 * by)
    if by > 0:
        return jnp.where(slot < 4 - by, turned, sub_roll(turned, -1))
    return jnp.where(slot >= -by, turned, sub_roll(turned, 1))


def factor(b):
    low = {}
    inv = [None] * 4
    for k in range(4):
        pivot = b[(k, k)]
        for m in range(k):
            if low.get((k, m)) is not None:
                pivot = pivot - low[(k, m)] * work[(k, m)]
        inv[k] = inverse(pivot, 2)
        if k == 0:
            work = {}
        for i in range(k + 1, 4):
            entry = b[(i, k)]
            for m in range(k):
                if low.get((i, m)) is None or work.get((k, m)) is None:
                    continue
                term = low[(i, m)] * work[(k, m)]
                entry = -term if entry is None else entry - term
            work[(i, k)] = entry
            low[(i, k)] = None if entry is None else entry * inv[k]
    return low, inv


def forward(low, column):
    out = []
    for i in range(4):
        value = column[i]
        for m in range(i):
            if low[(i, m)] is not None and out[m] is not None:
                term = low[(i, m)] * out[m]
                value = -term if value is None else value - term
        out.append(value)
    return out


def scaled(inv, column):
    return [None if v is None else v * inv[k] for k, v in enumerate(column)]


def inner(left, right):
    total = None
    for a, b in zip(left, right):
        if a is None or b is None:
            continue
        total = a * b if total is None else total + a * b
    return total


def subtract(value, term):
    if term is None:
        return value
    return -term if value is None else value - term


def shift_or_none(value, by, slot):
    return None if value is None else node_shift(value, by, slot)


def solve_nodes(b, c, d, slot):
    for step in (1, 2, 4, 8):
        a = [[shift_or_none(c[m][k], -step, slot) for m in range(4)] for k in range(4)]
        low, inv = factor(b)
        up = [forward(low, [c[i][k] for i in range(4)]) for k in range(4)]
        down = [forward(low, [a[i][k] for i in range(4)]) for k in range(4)]
        side = scaled(inv, forward(low, d))
        up_s = [scaled(inv, col) for col in up]
        down_s = [scaled(inv, col) for col in down]
        new_b = {}
        for i in range(4):
            for k in range(i + 1):
                value = subtract(b[(i, k)], shift_or_none(inner(up[i], up_s[k]), -step, slot))
                new_b[(i, k)] = subtract(value, shift_or_none(inner(down[i], down_s[k]), step, slot))
        new_d = []
        for i in range(4):
            value = subtract(d[i], shift_or_none(inner(up[i], side), -step, slot))
            new_d.append(subtract(value, shift_or_none(inner(down[i], side), step, slot)))
        new_c = [
            [subtract(None, shift_or_none(inner(down[i], up_s[k]), step, slot)) for k in range(4)]
            for i in range(4)
        ]
        b, c, d = new_b, new_c, new_d
    both = [[c[i][k] + node_shift(c[k][i], -16, slot) for k in range(4)] for i in range(4)]
    low, inv = factor(b)
    cols = [forward(low, [both[i][k] for i in range(4)]) for k in range(4)]
    cols_s = [scaled(inv, col) for col in cols]
    side = scaled(inv, forward(low, d))
    last = {}
    for i in range(4):
        for k in range(i + 1):
            last[(i, k)] = b[(i, k)] - node_shift(inner(cols[i], cols_s[k]), 16, slot)
    right = [d[i] - node_shift(inner(cols[i], side), 16, slot) for i in range(4)]
    low, inv = factor(last)
    value = scaled(inv, forward(low, right))
    for i in (2, 1, 0):
        for k in range(i + 1, 4):
            value[i] = value[i] - low[(k, i)] * value[k]
    return value


def corner_sums(g, r):
    k = [
        g[(3, 3)],
        g[(2, 3)] - g[(3, 3)],
        g[(1, 3)] - g[(3, 3)],
        g[(0, 3)] - g[(1, 3)] - g[(2, 3)] + g[(3, 3)],
        g[(2, 2)] - 2.0 * g[(2, 3)] + g[(3, 3)],
        g[(1, 2)] - g[(1, 3)] - g[(2, 3)] + g[(3, 3)],
        (g[(0, 2)] - g[(1, 2)] - g[(2, 2)]) + (2.0 * g[(2, 3)] - g[(0, 3)] + g[(1, 3)] - g[(3, 3)]),
        g[(1, 1)] - 2.0 * g[(1, 3)] + g[(3, 3)],
        (g[(0, 1)] - g[(1, 1)] - g[(1, 2)]) + (2.0 * g[(1, 3)] - g[(0, 3)] + g[(2, 3)] - g[(3, 3)]),
        (g[(0, 0)] + g[(1, 1)] + g[(2, 2)] + g[(3, 3)])
        - 2.0 * (g[(0, 1)] + g[(0, 2)] + g[(1, 3)] + g[(2, 3)] - g[(0, 3)] - g[(1, 2)]),
        r[3],
        r[2] - r[3],
        r[1] - r[3],
        r[0] - r[1] - r[2] + r[3],
    ]
    return k


GRAM = ((0, 0), (0, 1), (0, 2), (0, 3), (1, 1), (1, 2), (1, 3), (2, 2), (2, 3), (3, 3))


def assemble(t, slot):
    def back(value):
        return node_shift(value, -1, slot)

    b, d = {}, []
    c = [[None] * 4 for _ in range(4)]
    for i in range(4):
        w = (i - 1) % 4
        b[(i, i)] = t[0][i] + t[4][w] + back(t[7][i] + t[9][w])
        d.append(t[10][i] + t[11][w] + back(t[12][i] + t[13][w]))
        edge = t[1][i] + back(t[8][i])
        e = (i + 1) % 4
        b[(max(i, e), min(i, e))] = edge
        c[i][i] = t[2][i] + t[6][w]
        c[i][e] = t[3][i]
        c[e][i] = t[5][i]
    b[(2, 0)] = None
    b[(3, 1)] = None
    return b, c, d


def kernel(
    perm, accum, source, vtrans, press_out, resid_out,
    hx, ax, sx, vt, row24, row8, lo_out, hi_out, lo_n, lo_ne0, lo_ne1, lo_nw, hi_s, hi_se, hi_sw,
    tp, first_rows, ta, ts, teq, tnq, bq, tew, tnw, bw, tem, tnm, co, wt, sums, ga, nodes, cb, pu, pm, hm, yp, yh, po, ro,
    up_layer, down_pair, ready,
    local_sem, send_sem, recv_sem, gsend_sem, grecv_sem, vsend_sem, vrecv_sem, out_sem,
):
    gx, gy, gz = lax.axis_index("gx"), lax.axis_index("gy"), lax.axis_index("gz")

    def peer(dx, dy, dz):
        return (
            lax.rem(gx + (dx + SIDE), SIDE),
            lax.rem(gy + (dy + SIDE), SIDE),
            lax.rem(gz + (dz + DEPTH), DEPTH),
        )

    local = []

    def load(src, dst):
        copy = pltpu.make_async_copy(src, dst, local_sem.at[len(local)])
        copy.start()
        local.append(copy)

    for src, dst, first in ((perm, hx, 1), (accum, ax, 0), (source, sx, 0)):
        for half in range(2):
            load(src.at[pl.ds(24, 8), half], dst.at[first + half, pl.ds(0, 8)])
            load(src.at[pl.ds(0, 24), half], dst.at[first + half, pl.ds(8, 24)])
    load(vtrans, vt)

    has_below, has_above = gz > 0, gz < DEPTH - 1
    first_to_above = has_above & (gz != MIDDLE - 1)
    first_to_below = gz == MIDDLE
    next_to_above = gz == MIDDLE - 1
    next_to_below = has_below & (gz != MIDDLE)
    barrier = pltpu.get_barrier_semaphore()
    for dx in range(SIDE):
        for dy in range(SIDE):
            if dx or dy:
                pl.semaphore_signal(barrier, inc=1, device_id=peer(dx, dy, 0), device_id_type=MESH)
    for dz, there in ((-1, first_to_below), (1, first_to_above)):

        @pl.when(there)
        def _():
            pl.semaphore_signal(barrier, inc=1, device_id=peer(0, 0, dz), device_id_type=MESH)

    row = lax.broadcasted_iota(jnp.int32, (8, 128), 0)
    lane = lax.broadcasted_iota(jnp.int32, (8, 128), 1)
    group = lane // 16
    slot_of = lane // 32
    lower = lane < 64
    u_base = jnp.where(group % 2 == 1, 8, 0)
    row0 = row == 0
    row7 = row == 7
    u0 = u_base == 0
    u8 = u_base == 8

    for x in range(8):
        for p in range(2):
            w_x = 1.0 - (u_base + x).astype(F32) / 16.0
            w_y = 1.0 - (2 * row + p).astype(F32) / 16.0
            wt[0, x, p] = w_x
            wt[1, x, p] = w_y
            wt[2, x, p] = w_x * w_y

    hx_rows = hx.reshape(4 * 256, 128)
    ax_rows = ax.reshape(3 * 256, 128)
    sx_rows = sx.reshape(3 * 256, 128)

    def edges(rows, base, at_row, depth, with_high):
        for s in range(SETS):
            for half in range(2):
                first = base + 256 * half + 128 * s
                turned = jnp.concatenate([rows[pl.ds(first + x, 16, stride=8), :] for x in range(8)], axis=0).T
                lo_out[s, half, pl.ds(at_row, depth), :] = turned[:depth]
                if with_high:
                    hi_out[s, half] = turned[120:]

    for copy in local[:4]:
        copy.wait()
    row8[...] = hx_rows[pl.ds(512, LAYERS, stride=8), :]
    edges(hx_rows, 256, 0, 16, True)
    for copy in local[4:]:
        copy.wait()
    edges(ax_rows, 0, 16, 8, False)
    edges(sx_rows, 0, 24, 8, False)

    pl.semaphore_wait(barrier, 15 + next_to_above.astype(jnp.int32) + next_to_below.astype(jnp.int32))

    west, east = peer(-1, 0, 0), peer(1, 0, 0)
    south, north = peer(0, -1, 0), peer(0, 1, 0)

    def halo(s, first=0, end=12):
        mine = pl.ds(16 * s, 16)
        routes = (
            (hx.at[1, mine], hx.at[3, mine], west),
            (row8.at[mine], row24.at[mine], west),
            (lo_out.at[s], lo_n.at[s], south),
            (lo_out.at[s, 0], lo_ne0.at[s], peer(-1, -1, 0)),
            (lo_out.at[s, 1, pl.ds(0, 16)], lo_ne1.at[s], peer(-1, -1, 0)),
            (ax.at[0, mine], ax.at[2, mine], west),
            (sx.at[0, mine], sx.at[2, mine], west),
            (hx.at[2, mine], hx.at[0, mine], east),
            (lo_out.at[s, 1, pl.ds(0, 16)], lo_nw.at[s], peer(1, -1, 0)),
            (hi_out.at[s], hi_s.at[s], north),
            (hi_out.at[s], hi_se.at[s], peer(-1, 1, 0)),
            (hi_out.at[s, 1], hi_sw.at[s], peer(1, 1, 0)),
        )
        return [
            pltpu.make_async_remote_copy(
                src_ref=src, dst_ref=dst, send_sem=send_sem.at[s, i], recv_sem=recv_sem.at[s, i],
                device_id=target, device_id_type=MESH,
            )
            for i, (src, dst, target) in enumerate(routes)
            if first <= i < end
        ]

    def sums_messages(s):
        copies = []
        for dx in range(SIDE):
            for dy in range(SIDE):
                if dx or dy:
                    slot = (-dx % SIDE) * SIDE + (-dy % SIDE)
                    copies.append(
                        pltpu.make_async_remote_copy(
                            src_ref=ga.at[s, 0], dst_ref=ga.at[s, slot],
                            send_sem=gsend_sem.at[s, slot], recv_sem=grecv_sem.at[s, slot],
                            device_id=peer(dx, dy, 0), device_id_type=MESH,
                        )
                    )
        return copies

    for copy in halo(0, 0, 7):
        copy.start()
    for dz, at, there in ((-1, 0, next_to_below), (1, 1, next_to_above)):

        @pl.when(there)
        def _():
            pl.semaphore_signal(ready.at[at], inc=1, device_id=peer(0, 0, dz), device_id_type=MESH)

    def pick(at_group, left, by_left, right, by_right):
        return jnp.where(group == at_group, lane_roll(left, by_left), lane_roll(right, by_right))

    def turn(rows, first, second, fixed=None):
        part = [rows[pl.ds(first, 16, stride=8), :]]
        part.append(fixed if fixed is not None else rows[pl.ds(second, 16, stride=8), :])
        return jnp.concatenate(part * 4, axis=0).T

    def by_slot(load_slot):
        value = load_slot(3)
        for slot in (2, 1, 0):
            value = jnp.where(slot_of == slot, load_slot(slot), value)
        return value

    def relax(most, last, at, step, put_t, put_b):
        def cell(x, off):
            return by_slot(
                lambda slot: tp[last if slot == 3 else most, x, pl.ds(at + step * slot + off, 8, stride=2), :]
            )

        cells = [[cell(x, p) for p in range(2)] for x in range(9)]
        t_e = [[harmonic(cells[x][p], cells[x + 1][p]) for p in range(2)] for x in range(8)]
        for x in range(8):
            t_n = [harmonic(cells[x][0], cells[x][1]), harmonic(cells[x][1], cell(x, 2))]
            t_s = [sub_roll(t_n[1], 1), t_n[0]]
            for p in range(2):
                t_w = t_e[x - 1][p] if x else lane_roll(t_e[7][p], 1)
                put_t(x, p, t_e[x][p], t_n[p])
                inv = inverse((t_w + t_e[x][p]) + (t_s[p] + t_n[p]))
                if p == 0 and x == 0:
                    inv = jnp.where(row0 | u0, 0.0, inv)
                elif p == 0:
                    inv = jnp.where(row0, 0.0, inv)
                elif x == 0:
                    inv = jnp.where(u0, 0.0, inv)
                co[0, x, p] = t_w * inv
                co[1, x, p] = t_e[x][p] * inv
                co[2, x, p] = t_s[p] * inv
                co[3, x, p] = t_n[p] * inv

        def sweep(vals):
            new = []
            for x in range(8):
                pair = []
                for p in range(2):
                    west_v = vals[x - 1][p] if x else lane_roll(vals[7][p], 1)
                    east_v = vals[x + 1][p] if x < 7 else lane_roll(vals[0][p], -1)
                    south_v = vals[x][0] if p else sub_roll(vals[x][1], 1)
                    north_v = sub_roll(vals[x][0], -1) if p else vals[x][1]
                    pair.append(
                        (co[0, x, p] * west_v + co[1, x, p] * east_v) + (co[2, x, p] * south_v + co[3, x, p] * north_v)
                    )
                new.append(pair)
            return new

        def plus(left, right):
            return [[left[x][p] + right[x][p] for p in range(2)] for x in range(8)]

        for kind in range(3):
            push = []
            for x in range(8):
                pair = []
                for p in range(2):
                    w_x, w_y = wt[0, x, p], wt[1, x, p]
                    if kind == LX:
                        value = co[0, x, p] - co[1, x, p]
                    elif kind == LY:
                        value = co[2, x, p] - co[3, x, p]
                    else:
                        value = (co[0, x, p] - co[1, x, p]) * w_y + (co[2, x, p] - co[3, x, p]) * w_x
                    pair.append(value)
                push.append(pair)
            vals = plus(push, sweep(push))
            vals = plus(vals, sweep(sweep(vals)))
            vals = plus(vals, sweep(sweep(sweep(sweep(vals)))))
            for x in range(8):
                for p in range(2):
                    put_b(kind, x, p, wt[kind, x, p] + vals[x][p] * (1.0 / 16.0))

    def gram(s, e):
        at = 8 + 64 * e

        def load_packed(ref, x, p):
            return by_slot(lambda slot: ref[x, pl.ds(at + 16 * slot + p, 8, stride=2), :])

        acc = {}

        def add(key, value):
            acc[key] = value if key not in acc else acc[key] + value

        for x in range(8):
            for p in range(2):
                a = load_packed(ta, x, p)
                src = load_packed(ts, x, p)
                here = [bq[s, kind, e, x, p] for kind in range(3)]
                t_e, t_n = teq[s, e, x, p], tnq[s, e, x, p]
                mass, d_e, d_n = [], [], []
                for kind in range(3):
                    if x < 7:
                        east_v = bq[s, kind, e, x + 1, p]
                    else:
                        east_v = lane_roll(bq[s, kind, e, 0, p], -1)
                        if kind != LY:
                            east_v = jnp.where(u8, 0.0, east_v)
                    if p:
                        north_v = sub_roll(bq[s, kind, e, x, 0], -1)
                        if kind != LX:
                            north_v = jnp.where(row7, 0.0, north_v)
                    else:
                        north_v = bq[s, kind, e, x, 1]
                    d_e.append(here[kind] - east_v)
                    d_n.append(here[kind] - north_v)
                    mass.append(a * here[kind])
                add((0, 0), a)
                add("r0", src)
                for kind in range(3):
                    add((0, kind + 1), mass[kind])
                    add("r" + str(kind + 1), src * here[kind])
                    w_e, w_n = t_e * d_e[kind], t_n * d_n[kind]
                    for other in range(kind, 3):
                        add((kind + 1, other + 1), mass[kind] * here[other] + w_e * d_e[other] + w_n * d_n[other])
        for index, key in enumerate(GRAM + ("r0", "r1", "r2", "r3")):
            value = acc[key]
            value = value + sub_roll(value, 4)
            value = value + sub_roll(value, 2)
            value = value + sub_roll(value, 1)
            sums[e, index] = value + lane_roll(value, -1)

    def owned(s, carry):
        copies = halo(s, 0, 7)
        copies[0].wait_recv()
        copies[1].wait_recv()

        @pl.when(s == 0)
        def _():
            for copy in halo(1, 0, 7) + halo(0, 7):
                copy.start()

        @pl.when(s == 1)
        def _():
            for copy in halo(1, 7):
                copy.start()

        for x in range(9):
            if x < 8:
                value = turn(hx_rows, 512 + 128 * s + x, 768 + 128 * s + x)
            else:
                value = turn(hx_rows, 768 + 128 * s, None, row24[pl.ds(pl.multiple_of(16 * s, 16), 16), :])
            tp[1, x, pl.ds(8, 128), :] = value
            first_rows[s, x] = value[:16]
        for copy in copies[2:5]:
            copy.wait_recv()
        for t in range(2):
            at = pl.ds(8 * t, 8)
            for x in range(8):
                tp[1, x, pl.ds(136 + 8 * t, 8), :] = pick(6, lo_n[s, 1, at, :], 6 - x, lo_ne0[s, at, :], 7 - x)
            tp[1, 8, pl.ds(136 + 8 * t, 8), :] = pick(6, lo_ne0[s, at, :], 6, lo_ne1[s, at, :], 7)

        def unit(e, inner):
            def put_t(x, p, east_t, north_t):
                teq[s, e, x, p] = east_t
                tnq[s, e, x, p] = north_t

            def put_b(kind, x, p, value):
                bq[s, kind, e, x, p] = value

            relax(1, 1, 16 + 64 * e, 16, put_t, put_b)
            return inner

        lax.fori_loop(0, 2, unit, 0)

        copies[5].wait_recv()
        copies[6].wait_recv()
        for rows, turned, at_row in ((ax_rows, ta, 16), (sx_rows, ts, 24)):
            for x in range(8):
                turned[x, pl.ds(0, 128), :] = turn(rows, 256 + 128 * s + x, 512 + 128 * s + x)
                at = pl.ds(at_row, 8)
                turned[x, pl.ds(128, 8), :] = pick(6, lo_n[s, 1, at, :], 6 - x, lo_ne0[s, at, :], 7 - x)

        def one(e, inner):
            gram(s, e)
            return inner

        lax.fori_loop(0, 2, one, 0)

        whole = []
        for index in range(14):
            whole.append(jnp.where(row % 2 == 0, sums[0, index], sums[1, index]))
        entries = corner_sums({key: whole[i] for i, key in enumerate(GRAM)}, whole[10:])
        for m in range(2):
            packed = jnp.zeros((8, 128), F32)
            for t in range(4 * m, min(4 * m + 4, 7)):
                pair = jnp.where(group % 2 == 0, entries[2 * t], lane_roll(entries[2 * t + 1], 1))
                packed = jnp.where(row // 2 == t % 4, pair, packed)
            ga[s, 0, m] = packed
        for copy in sums_messages(s):
            copy.start()
        return carry

    lax.fori_loop(0, SETS, owned, 0)

    def merge(left, right):
        inner = lane_roll(jnp.where(slot_of == 0, right, left), 2)
        outer = lane_roll(jnp.where(slot_of == 1, right, left), 4)
        upper = lane_roll(jnp.where(slot_of == 2, right, left), -2)
        ends = (slot_of == 1) | (slot_of == 2)
        first = jnp.where(slot_of == 0, left, jnp.where(ends, inner, outer))
        second = jnp.where(slot_of == 3, right, jnp.where(ends, upper, outer))
        return first, second

    def to_rows(s, merged, lines, dst):
        for k in range(5):
            for which in range(2):
                if k == 0 and which == 0:
                    continue
                for p in range(2):
                    for part in range(2):
                        value = None
                        for q in range(4):
                            moved = lane_roll(merged[k, 4 * part + q, p], 2 * q - 1 - 4 * which)
                            value = moved if value is None else jnp.where(slot_of == q, moved, value)
                        lines[part, pl.ds(16 * (2 * k - 1 + which) + p, 8, stride=2), :] = value
        for part in range(2):
            turned = lines[part, pl.ds(8, 128), :].T
            for q in range(4):
                for half in range(2):
                    for b in range(2):
                        first = 32 * q + 16 * half + 8 * b
                        layer = lax.rem(16 * s + (8 * b + 24), LAYERS)
                        dst[pl.ds(16 * layer + (8 * half + 4 * part + q), 8, stride=16), :] = turned[first : first + 8]

    low_send = pltpu.make_async_remote_copy(
        src_ref=po.at[pl.ds(0, 16)], dst_ref=up_layer, send_sem=vsend_sem.at[0], recv_sem=vrecv_sem.at[0],
        device_id=peer(0, 0, -1), device_id_type=MESH,
    )
    high_send = pltpu.make_async_remote_copy(
        src_ref=po.at[pl.ds(496, 16)], dst_ref=down_pair.at[0], send_sem=vsend_sem.at[1], recv_sem=vrecv_sem.at[1],
        device_id=peer(0, 0, 1), device_id_type=MESH,
    )
    vt_up = pltpu.make_async_remote_copy(
        src_ref=vt.at[pl.ds(496, 16)], dst_ref=down_pair.at[1], send_sem=vsend_sem.at[2], recv_sem=vrecv_sem.at[2],
        device_id=peer(0, 0, 1), device_id_type=MESH,
    )

    def rest(s, carry):
        for copy in halo(s, 7):
            copy.wait_recv()
        for x in range(9):
            if x < 8:
                value = turn(hx_rows, 128 * s + x, 256 + 128 * s + x)
            else:
                value = turn(hx_rows, 256 + 128 * s, 512 + 128 * s)
            tp[0, x, pl.ds(8, 128), :] = value
            tp[1, x, pl.ds(8, 16), :] = first_rows[s, x]
        for x in range(8):
            for t in range(2):
                at = pl.ds(8 * t, 8)
                tp[0, x, pl.ds(136 + 8 * t, 8), :] = pick(6, lo_nw[s, at, :], 6 - x, lo_n[s, 0, at, :], 7 - x)
            tp[0, x, pl.ds(0, 8), :] = pick(4, hi_sw[s], 4 - x, hi_s[s, 0], 5 - x)
            tp[1, x, pl.ds(0, 8), :] = pick(6, hi_s[s, 1], 6 - x, hi_se[s, 0], 7 - x)
        for t in range(2):
            at = pl.ds(8 * t, 8)
            tp[0, 8, pl.ds(136 + 8 * t, 8), :] = pick(6, lo_n[s, 0, at, :], 6, lo_n[s, 1, at, :], 7)
        tp[0, 8, pl.ds(0, 8), :] = pick(4, hi_s[s, 0], 4, hi_s[s, 1], 5)
        tp[1, 8, pl.ds(0, 8), :] = pick(6, hi_se[s, 0], 6, hi_se[s, 1], 7)

        def unit(e, inner):
            edge = e // 2

            def put_t(x, p, east_t, north_t):
                tew[e, x, p] = east_t
                tnw[e, x, p] = north_t

            def put_b(kind, x, p, value):
                bw[kind, e, x, p] = value

            relax(0, edge, (16 + 64 * e) * (1 - edge), 16 * (1 - edge), put_t, put_b)
            return inner

        lax.fori_loop(0, 3, unit, 0)
        tem[0] = tew[2]
        tnm[0] = tnw[2]

        def merge_t(e, inner):
            for x in range(8):
                for p in range(2):
                    for left, right, out in ((tew, teq, tem), (tnw, tnq, tnm)):
                        first, second = merge(left[e, x, p], right[s, e, x, p])
                        out[1 + 2 * e, x, p] = first
                        out[2 + 2 * e, x, p] = second
            return inner

        lax.fori_loop(0, 2, merge_t, 0)

        for copy in sums_messages(s):
            copy.wait()
        table = []
        for t in range(7):
            even, odd = [], []
            for i in range(SIDE):
                value = None
                for g in range(SIDE):
                    moved = sub_roll(ga[s, i * SIDE + g, t // 4], 2 * g - 2 * (t % 4))
                    value = moved if value is None else jnp.where(row // 2 == g, moved, value)
                even.append(jnp.where(group % 2 == 0, value, lane_roll(value, 1)))
                odd.append(jnp.where(group % 2 == 1, value, lane_roll(value, -1)))
            table.append(even)
            table.append(odd)
        b, c, d_side = assemble(table, slot_of)
        coarse = solve_nodes(b, c, d_side, slot_of)

        for place, i in enumerate((3, 0, 1)):
            nodes[0, place] = coarse[i]
            nodes[1, place] = node_shift(coarse[i], 1, slot_of)

        def line(by, place, j):
            return jnp.broadcast_to(nodes[by, place, pl.ds(j, 1), :], (8, 128))

        def put_weights(unit_at, c0, c1, c2, c3):
            cb[unit_at, 0] = c3
            cb[unit_at, 1] = c2 - c3
            cb[unit_at, 2] = c1 - c3
            cb[unit_at, 3] = (c0 - c1) - (c2 - c3)

        for e in range(2):
            near = [line(0, place, e) for place in range(3)]
            far = [line(1, place, e) for place in range(3)]
            put_weights(e, near[1], near[2], far[1], far[2])
            put_weights(2 + e, near[0], near[1], far[0], far[1])
        last = slot_of == 3
        below = [line(0, place, 7) for place in range(3)]
        first = [line(0, place, 0) for place in range(3)]
        put_weights(
            4,
            *(jnp.where(last, below[k + 1], lane_roll(below[k], -2)) for k in range(2)),
            *(jnp.where(last, lane_roll(first[k + 1], 6), lane_roll(first[k], 4)) for k in range(2)),
        )

        def pressures(w, basis_at, x, p):
            return (w[0] + w[1] * basis_at(0, x, p)) + (w[2] * basis_at(1, x, p) + w[3] * basis_at(2, x, p))

        def interpolate(e, inner):
            w_own = [cb[e, k] for k in range(4)]
            w_west = [cb[2 + e, k] for k in range(4)]
            for x in range(8):
                for p in range(2):
                    own = pressures(w_own, lambda kind, x, p: bq[s, kind, e, x, p], x, p)
                    other = pressures(w_west, lambda kind, x, p: bw[kind, e, x, p], x, p)
                    first, second = merge(other, own)
                    pm[1 + 2 * e, x, p] = first
                    pm[2 + 2 * e, x, p] = second
            return inner

        lax.fori_loop(0, 2, interpolate, 0)
        w_edge = [cb[4, k] for k in range(4)]
        for x in range(8):
            for p in range(2):
                pm[0, x, p] = pressures(w_edge, lambda kind, x, p: bw[kind, 2, x, p], x, p)
        to_rows(s, pm, yp, po)

        @pl.when((s == 0) & first_to_above)
        def _():
            pl.semaphore_wait(ready.at[0], 1)

        @pl.when((s == 0) & has_above)
        def _():
            high_send.start()
            vt_up.start()

        @pl.when((s == 0) & first_to_below)
        def _():
            pl.semaphore_wait(ready.at[1], 1)

        @pl.when((s == 0) & has_below)
        def _():
            low_send.start()

        def balance(k, inner):
            val = [[pm[k, x, p] for p in range(2)] for x in range(8)]
            f_e = [[None, None] for _ in range(8)]
            for x in range(8):
                for p in range(2):
                    east_v = val[x + 1][p] if x < 7 else lane_roll(val[0][p], -1)
                    f_e[x][p] = tem[k, x, p] * (val[x][p] - east_v)
            for x in range(8):
                after = lane_roll(jnp.where(lower, pm[k + 1, x, 0], val[x][0]), 4)
                after = sub_roll(jnp.where(row0, after, val[x][0]), -1)
                f_n0 = tnm[k, x, 0] * (val[x][0] - val[x][1])
                f_n1 = tnm[k, x, 1] * (val[x][1] - after)
                before = lane_roll(jnp.where(lower, f_n1, pu[x]), 4)
                before = sub_roll(jnp.where(row7, before, f_n1), 1)
                pu[x] = f_n1
                f_n = (f_n0, f_n1)
                f_s = (before, f_n0)
                for p in range(2):
                    f_w = f_e[x - 1][p] if x else lane_roll(f_e[7][p], 1)
                    hm[k, x, p] = (f_e[x][p] - f_w) + (f_n[p] - f_s[p])
            return inner

        lax.fori_loop(0, 5, balance, 0)
        to_rows(s, hm, yh, ro)
        return carry

    lax.fori_loop(0, SETS, rest, 0)
    press_copy = pltpu.make_async_copy(po, press_out, out_sem.at[0])
    press_copy.start()

    for half in range(2):
        before = None
        for l in range(LAYERS):
            at = pl.ds(16 * l + 8 * half, 8)
            place = (l + 8) % LAYERS
            here = po[at, :]
            value = sx[half, place] - ax[half, place] * here - ro[at, :]
            if before is not None:
                value = value + before
            if l < LAYERS - 1:
                before = vt[at, :] * (here - po[pl.ds(16 * (l + 1) + 8 * half, 8), :])
                value = value - before
            ro[at, :] = value

    middle_copy = pltpu.make_async_copy(ro.at[pl.ds(16, 480)], resid_out.at[pl.ds(16, 480)], out_sem.at[1])
    middle_copy.start()
    for s in range(SETS):
        for copy in halo(s):
            copy.wait_send()
    press_copy.wait()

    @pl.when(has_below)
    def _():
        vt_up.wait_recv()
        high_send.wait_recv()
        low_send.wait_send()

    @pl.when(has_above)
    def _():
        low_send.wait_recv()
        high_send.wait_send()
        vt_up.wait_send()

    above = jnp.where(has_above, vt[pl.ds(496, 16), :] * (po[pl.ds(496, 16), :] - up_layer[...]), 0.0)
    below = jnp.where(has_below, down_pair[1] * (down_pair[0] - po[pl.ds(0, 16), :]), 0.0)
    ro[pl.ds(496, 16), :] = ro[pl.ds(496, 16), :] - above
    ro[pl.ds(0, 16), :] = ro[pl.ds(0, 16), :] + below
    edge_copies = [
        pltpu.make_async_copy(ro.at[pl.ds(at, 16)], resid_out.at[pl.ds(at, 16)], out_sem.at[2 + i])
        for i, at in enumerate((0, 496))
    ]
    for copy in edge_copies:
        copy.start()
    middle_copy.wait()
    for copy in edge_copies:
        copy.wait()


def body(permeability, accumulation, source_term, vertical_trans):
    split = (LAYERS, 2, 8, 128)
    vmem = lambda *shape: pltpu.VMEM(shape, F32)
    anywhere = pl.BlockSpec(memory_space=pl.ANY)
    in_hbm = pl.BlockSpec(memory_space=pltpu.HBM)
    pressure, residual = pl.pallas_call(
        kernel,
        out_shape=[jax.ShapeDtypeStruct((512, 128), F32)] * 2,
        in_specs=[in_hbm] * 4,
        out_specs=[anywhere] * 2,
        scratch_shapes=[
            vmem(4, 32, 8, 128),
            vmem(3, 32, 8, 128),
            vmem(3, 32, 8, 128),
            vmem(512, 128),
            vmem(32, 128),
            vmem(32, 128),
            vmem(2, 2, 32, 128),
            vmem(2, 2, 8, 128),
            vmem(2, 2, 32, 128),
            vmem(2, 32, 128),
            vmem(2, 16, 128),
            vmem(2, 16, 128),
            vmem(2, 2, 8, 128),
            vmem(2, 2, 8, 128),
            vmem(2, 8, 128),
            vmem(2, 9, 152, 128),
            vmem(2, 9, 16, 128),
            vmem(8, 136, 128),
            vmem(8, 136, 128),
            vmem(2, 2, 8, 2, 8, 128),
            vmem(2, 2, 8, 2, 8, 128),
            vmem(2, 3, 2, 8, 2, 8, 128),
            vmem(3, 8, 2, 8, 128),
            vmem(3, 8, 2, 8, 128),
            vmem(3, 3, 8, 2, 8, 128),
            vmem(5, 8, 2, 8, 128),
            vmem(5, 8, 2, 8, 128),
            vmem(4, 8, 2, 8, 128),
            vmem(3, 8, 2, 8, 128),
            vmem(2, 14, 8, 128),
            vmem(2, 16, 2, 8, 128),
            vmem(2, 3, 8, 128),
            vmem(5, 4, 8, 128),
            vmem(8, 8, 128),
            vmem(6, 8, 2, 8, 128),
            vmem(5, 8, 2, 8, 128),
            vmem(2, 144, 128),
            vmem(2, 144, 128),
            vmem(512, 128),
            vmem(512, 128),
            vmem(16, 128),
            vmem(2, 16, 128),
            pltpu.SemaphoreType.REGULAR((2,)),
            pltpu.SemaphoreType.DMA((13,)),
            pltpu.SemaphoreType.DMA((2, 12)),
            pltpu.SemaphoreType.DMA((2, 12)),
            pltpu.SemaphoreType.DMA((2, 16)),
            pltpu.SemaphoreType.DMA((2, 16)),
            pltpu.SemaphoreType.DMA((3,)),
            pltpu.SemaphoreType.DMA((3,)),
            pltpu.SemaphoreType.DMA((4,)),
        ],
        compiler_params=pltpu.CompilerParams(
            collective_id=0, has_side_effects=True, vmem_limit_bytes=40 * 1024 * 1024
        ),
    )(
        *(
            pltpu.with_memory_space_constraint(value, pltpu.HBM)
            for value in (
                permeability.reshape(split),
                accumulation.reshape(split),
                source_term.reshape(split),
                vertical_trans.reshape(512, 128),
            )
        ),
    )
    return pressure.reshape(32, 16, 128), residual.reshape(32, 16, 128)


def solution(mesh):
    spec = P("gz", "gx", "gy")
    return jax.shard_map(
        body, mesh=mesh, in_specs=(spec,) * 4, out_specs=(spec, spec), check_vma=False
    )
```

time: 31.2 us -> 29.8 us (0.955)
  Pallas kernels: 29.1 us -> 27.6 us
    pallas_call x1, Pallas kernels: 29.1 us -> 27.6 us  [body(): pl.pallas_call(kernel, out_shape=[jax.ShapeDtypeStruct((512, 128), F32)]...]
where the time goes in v3:
time: 29.8 us; the launch traced here: 29.7 us
  Pallas kernels  27.6 us (93%)
  local copies, waits for them, and re-layouts  1.41 us (5%)
  between operations  0.64 us (2%)
    pallas_call x1, Pallas kernels, body(): pl.pallas_call(kernel, out_shape=[jax.ShapeDtypeStruct((512, 128), F32)]...  27.6 us
    unnamed x2, local copies, waits for them, and re-layouts  1.41 us

profile of v3, /device:TPU:25, one launch (start us, length us, event | category | flops | bytes accessed | tf_op | source)
XLA Modules:
  0.0 29.7 jit_solution(11171282589127960078)
XLA Ops:
  0.6 27.6 %shard_map.59 = (f32[512,128]{1,0:T(8,128)S(1)}, f32[512,128]{1,0:T(8,128)S(1)}) custom-call(f32[32,2,8,128]{3,2,1,0:T(8,128)} %bitcast.8, f32[32,2,8,128]{3,2,1,0:T(8,128)} %bitcast.9, f32[32,2,8,128]{3,2,1,0:T(8,128)} %bitcast.10, f32[512,128]{1,0:T(8,128)} %bitcast.11), custom_call_target="tpu_custom_call" | custom-call | tf_op jit(solution)/shard_map/pallas_call | solution.py:791
  28.3 0.7 %copy.8 = f32[32,16,128]{2,1,0:T(8,128)} copy(f32[32,16,128]{2,1,0:T(8,128)S(1)} %bitcast.7) | data formatting | bytes 524288
  29.0 0.7 %copy.9 = f32[32,16,128]{2,1,0:T(8,128)} copy(f32[32,16,128]{2,1,0:T(8,128)S(1)} %bitcast.6) | data formatting | bytes 524288

commit v4 on v3

--- a/solution.py
+++ b/solution.py
@@ -192,7 +192,7 @@
 def kernel(
     perm, accum, source, vtrans, press_out, resid_out,
     hx, ax, sx, vt, row24, row8, lo_out, hi_out, lo_n, lo_ne0, lo_ne1, lo_nw, hi_s, hi_se, hi_sw,
-    tp, first_rows, ta, ts, teq, tnq, bq, tew, tnw, bw, tem, tnm, co, wt, sums, ga, nodes, cb, pu, pm, hm, yp, yh, po, ro,
+    tp, first_rows, ta, ts, teq, tnq, bq, tew, tnw, bw, tem, tnm, co, wt, sums, ga, nodes, cb, pu, ends, pm, hm, yp, yh, po, ro,
     up_layer, down_pair, ready,
     local_sem, send_sem, recv_sem, gsend_sem, grecv_sem, vsend_sem, vrecv_sem, out_sem,
 ):
@@ -204,19 +204,6 @@
             lax.rem(gy + (dy + SIDE), SIDE),
             lax.rem(gz + (dz + DEPTH), DEPTH),
         )
-
-    local = []
-
-    def load(src, dst):
-        copy = pltpu.make_async_copy(src, dst, local_sem.at[len(local)])
-        copy.start()
-        local.append(copy)
-
-    for src, dst, first in ((perm, hx, 1), (accum, ax, 0), (source, sx, 0)):
-        for half in range(2):
-            load(src.at[pl.ds(24, 8), half], dst.at[first + half, pl.ds(0, 8)])
-            load(src.at[pl.ds(0, 24), half], dst.at[first + half, pl.ds(8, 24)])
-    load(vtrans, vt)
 
     has_below, has_above = gz > 0, gz < DEPTH - 1
     first_to_above = has_above & (gz != MIDDLE - 1)
@@ -234,6 +221,19 @@
         def _():
             pl.semaphore_signal(barrier, inc=1, device_id=peer(0, 0, dz), device_id_type=MESH)
 
+    local = []
+
+    def load(src, dst):
+        copy = pltpu.make_async_copy(src, dst, local_sem.at[len(local)])
+        copy.start()
+        local.append(copy)
+
+    for src, dst, first in ((perm, hx, 1), (accum, ax, 0), (source, sx, 0)):
+        for half in range(2):
+            load(src.at[pl.ds(24, 8), half], dst.at[first + half, pl.ds(0, 8)])
+            load(src.at[pl.ds(0, 24), half], dst.at[first + half, pl.ds(8, 24)])
+    load(vtrans, vt)
+
     row = lax.broadcasted_iota(jnp.int32, (8, 128), 0)
     lane = lax.broadcasted_iota(jnp.int32, (8, 128), 1)
     group = lane // 16
@@ -269,12 +269,6 @@
     for copy in local[:4]:
         copy.wait()
     row8[...] = hx_rows[pl.ds(512, LAYERS, stride=8), :]
-    edges(hx_rows, 256, 0, 16, True)
-    for copy in local[4:]:
-        copy.wait()
-    edges(ax_rows, 0, 16, 8, False)
-    edges(sx_rows, 0, 24, 8, False)
-
     pl.semaphore_wait(barrier, 15 + next_to_above.astype(jnp.int32) + next_to_below.astype(jnp.int32))
 
     west, east = peer(-1, 0, 0), peer(1, 0, 0)
@@ -320,7 +314,16 @@
                     )
         return copies
 
-    for copy in halo(0, 0, 7):
+    for copy in halo(0, 0, 2):
+        copy.start()
+    for copy in local[4:]:
+        copy.wait()
+    for copy in halo(0, 5, 7):
+        copy.start()
+    edges(hx_rows, 256, 0, 16, True)
+    edges(ax_rows, 0, 16, 8, False)
+    edges(sx_rows, 0, 24, 8, False)
+    for copy in halo(0, 2, 5):
         copy.start()
     for dz, at, there in ((-1, 0, next_to_below), (1, 1, next_to_above)):
 
@@ -368,44 +371,43 @@
                 co[2, x, p] = t_s[p] * inv
                 co[3, x, p] = t_n[p] * inv
 
-        def sweep(vals):
-            new = []
-            for x in range(8):
-                pair = []
+        def sweep(kinds):
+            new = [[[None, None] for _ in range(8)] for _ in kinds]
+            for x in (0, 7, 1, 6, 2, 5, 3, 4):
                 for p in range(2):
-                    west_v = vals[x - 1][p] if x else lane_roll(vals[7][p], 1)
-                    east_v = vals[x + 1][p] if x < 7 else lane_roll(vals[0][p], -1)
-                    south_v = vals[x][0] if p else sub_roll(vals[x][1], 1)
-                    north_v = sub_roll(vals[x][0], -1) if p else vals[x][1]
-                    pair.append(
-                        (co[0, x, p] * west_v + co[1, x, p] * east_v) + (co[2, x, p] * south_v + co[3, x, p] * north_v)
-                    )
-                new.append(pair)
+                    c_w, c_e, c_s, c_n = (co[i, x, p] for i in range(4))
+                    for vals, out in zip(kinds, new):
+                        west_v = vals[x - 1][p] if x else lane_roll(vals[7][p], 1)
+                        east_v = vals[x + 1][p] if x < 7 else lane_roll(vals[0][p], -1)
+                        south_v = vals[x][0] if p else sub_roll(vals[x][1], 1)
+                        north_v = sub_roll(vals[x][0], -1) if p else vals[x][1]
+                        out[x][p] = (c_w * west_v + c_e * east_v) + (c_s * south_v + c_n * north_v)
             return new
 
         def plus(left, right):
-            return [[left[x][p] + right[x][p] for p in range(2)] for x in range(8)]
-
-        for kind in range(3):
+            return [[[a[x][p] + b[x][p] for p in range(2)] for x in range(8)] for a, b in zip(left, right)]
+
+        for kinds in ((0, 1, 2),):
             push = []
-            for x in range(8):
-                pair = []
-                for p in range(2):
-                    w_x, w_y = wt[0, x, p], wt[1, x, p]
-                    if kind == LX:
-                        value = co[0, x, p] - co[1, x, p]
-                    elif kind == LY:
-                        value = co[2, x, p] - co[3, x, p]
-                    else:
-                        value = (co[0, x, p] - co[1, x, p]) * w_y + (co[2, x, p] - co[3, x, p]) * w_x
-                    pair.append(value)
-                push.append(pair)
+            for kind in kinds:
+                push.append([[None, None] for _ in range(8)])
+                for x in range(8):
+                    for p in range(2):
+                        w_x, w_y = wt[0, x, p], wt[1, x, p]
+                        if kind == LX:
+                            value = co[0, x, p] - co[1, x, p]
+                        elif kind == LY:
+                            value = co[2, x, p] - co[3, x, p]
+                        else:
+                            value = (co[0, x, p] - co[1, x, p]) * w_y + (co[2, x, p] - co[3, x, p]) * w_x
+                        push[-1][x][p] = value
             vals = plus(push, sweep(push))
             vals = plus(vals, sweep(sweep(vals)))
             vals = plus(vals, sweep(sweep(sweep(sweep(vals)))))
-            for x in range(8):
-                for p in range(2):
-                    put_b(kind, x, p, wt[kind, x, p] + vals[x][p] * (1.0 / 16.0))
+            for kind, done in zip(kinds, vals):
+                for x in range(8):
+                    for p in range(2):
+                        put_b(kind, x, p, wt[kind, x, p] + done[x][p] * (1.0 / 16.0))
 
     def gram(s, e):
         at = 8 + 64 * e
@@ -529,33 +531,35 @@
 
     lax.fori_loop(0, SETS, owned, 0)
 
-    def merge(left, right):
-        inner = lane_roll(jnp.where(slot_of == 0, right, left), 2)
-        outer = lane_roll(jnp.where(slot_of == 1, right, left), 4)
-        upper = lane_roll(jnp.where(slot_of == 2, right, left), -2)
-        ends = (slot_of == 1) | (slot_of == 2)
-        first = jnp.where(slot_of == 0, left, jnp.where(ends, inner, outer))
-        second = jnp.where(slot_of == 3, right, jnp.where(ends, upper, outer))
-        return first, second
-
-    def to_rows(s, merged, lines, dst):
-        for k in range(5):
-            for which in range(2):
-                if k == 0 and which == 0:
-                    continue
-                for p in range(2):
-                    for part in range(2):
-                        value = None
-                        for q in range(4):
-                            moved = lane_roll(merged[k, 4 * part + q, p], 2 * q - 1 - 4 * which)
-                            value = moved if value is None else jnp.where(slot_of == q, moved, value)
-                        lines[part, pl.ds(16 * (2 * k - 1 + which) + p, 8, stride=2), :] = value
+    even = group % 2 == 0
+    even_slot = slot_of % 2 == 0
+
+    def to_rows(s, tiles, lines, dst):
+        for part in range(2):
+            for p in range(2):
+                for e in range(2):
+                    a = [tiles[e, 4 * part + q, p] for q in range(4)]
+                    b = [None] * 4
+                    for q in range(2):
+                        crossed = lane_roll(jnp.where(lower, a[q + 2], a[q]), 4)
+                        b[q] = jnp.where(lower, a[q], crossed)
+                        b[q + 2] = jnp.where(lower, crossed, a[q + 2])
+                    for q in (0, 2):
+                        for slot, value in (
+                            (q, jnp.where(even_slot, b[q], lane_roll(b[q + 1], 2))),
+                            (q + 1, jnp.where(even_slot, lane_roll(b[q], -2), b[q + 1])),
+                        ):
+                            lines[part, pl.ds(16 * (1 + 4 * e + slot) + p, 8, stride=2), :] = value
+                value = tiles[2, 4 * part + 3, p]
+                for q in range(3):
+                    value = jnp.where(slot_of == q, lane_roll(tiles[2, 4 * part + q, p], 2 * (q - 3)), value)
+                lines[part, pl.ds(p, 8, stride=2), :] = value
         for part in range(2):
             turned = lines[part, pl.ds(8, 128), :].T
             for q in range(4):
                 for half in range(2):
                     for b in range(2):
-                        first = 32 * q + 16 * half + 8 * b
+                        first = 32 * q + 16 * (1 - half) + 8 * b
                         layer = lax.rem(16 * s + (8 * b + 24), LAYERS)
                         dst[pl.ds(16 * layer + (8 * half + 4 * part + q), 8, stride=16), :] = turned[first : first + 8]
 
@@ -608,34 +612,20 @@
             return inner
 
         lax.fori_loop(0, 3, unit, 0)
-        tem[0] = tew[2]
-        tnm[0] = tnw[2]
-
-        def merge_t(e, inner):
-            for x in range(8):
-                for p in range(2):
-                    for left, right, out in ((tew, teq, tem), (tnw, tnq, tnm)):
-                        first, second = merge(left[e, x, p], right[s, e, x, p])
-                        out[1 + 2 * e, x, p] = first
-                        out[2 + 2 * e, x, p] = second
-            return inner
-
-        lax.fori_loop(0, 2, merge_t, 0)
-
         for copy in sums_messages(s):
             copy.wait()
         table = []
         for t in range(7):
-            even, odd = [], []
+            pair = ([], [])
             for i in range(SIDE):
                 value = None
                 for g in range(SIDE):
                     moved = sub_roll(ga[s, i * SIDE + g, t // 4], 2 * g - 2 * (t % 4))
                     value = moved if value is None else jnp.where(row // 2 == g, moved, value)
-                even.append(jnp.where(group % 2 == 0, value, lane_roll(value, 1)))
-                odd.append(jnp.where(group % 2 == 1, value, lane_roll(value, -1)))
-            table.append(even)
-            table.append(odd)
+                pair[0].append(jnp.where(group % 2 == 0, value, lane_roll(value, 1)))
+                pair[1].append(jnp.where(group % 2 == 1, value, lane_roll(value, -1)))
+            table.append(pair[0])
+            table.append(pair[1])
         b, c, d_side = assemble(table, slot_of)
         coarse = solve_nodes(b, c, d_side, slot_of)
 
@@ -669,23 +659,48 @@
         def pressures(w, basis_at, x, p):
             return (w[0] + w[1] * basis_at(0, x, p)) + (w[2] * basis_at(1, x, p) + w[3] * basis_at(2, x, p))
 
+        def put_ends(k, east_0, west_7, west_0, t_west_7, p, by):
+            ends[k, 0, p] = jnp.where(even, lane_roll(east_0, -1), lane_roll(east_0, 1))
+            ends[k, 1, p] = lane_roll(t_west_7 * (west_7 - lane_roll(west_0, -1)), by)
+
         def interpolate(e, inner):
             w_own = [cb[e, k] for k in range(4)]
             w_west = [cb[2 + e, k] for k in range(4)]
-            for x in range(8):
-                for p in range(2):
-                    own = pressures(w_own, lambda kind, x, p: bq[s, kind, e, x, p], x, p)
-                    other = pressures(w_west, lambda kind, x, p: bw[kind, e, x, p], x, p)
-                    first, second = merge(other, own)
-                    pm[1 + 2 * e, x, p] = first
-                    pm[2 + 2 * e, x, p] = second
+            w_both = [jnp.where(even, a, b) for a, b in zip(w_own, w_west)]
+
+            def own(kind, x, p):
+                return bq[s, kind, e, x, p]
+
+            def other(kind, x, p):
+                return bw[kind, e, x, p]
+
+            def both(kind, x, p):
+                return jnp.where(even, bq[s, kind, e, x, p], bw[kind, e, x, p])
+
+            for p in range(2):
+                for x in range(8):
+                    pm[e, x, p] = pressures(w_both, both, x, p)
+                    tem[e, x, p] = jnp.where(even, teq[s, e, x, p], tew[e, x, p])
+                    tnm[e, x, p] = jnp.where(even, tnq[s, e, x, p], tnw[e, x, p])
+                put_ends(
+                    e, pressures(w_own, own, 0, p), pressures(w_west, other, 7, p),
+                    pressures(w_west, other, 0, p), tew[e, 7, p], p, 1,
+                )
             return inner
 
         lax.fori_loop(0, 2, interpolate, 0)
         w_edge = [cb[4, k] for k in range(4)]
-        for x in range(8):
-            for p in range(2):
-                pm[0, x, p] = pressures(w_edge, lambda kind, x, p: bw[kind, 2, x, p], x, p)
+
+        def to_own(value):
+            return jnp.where(even, value, lane_roll(value, 2))
+
+        for p in range(2):
+            edge = [pressures(w_edge, lambda kind, x, p: bw[kind, 2, x, p], x, p) for x in range(8)]
+            for x in range(8):
+                pm[2, x, p] = to_own(edge[x])
+                tem[2, x, p] = to_own(tew[2, x, p])
+                tnm[2, x, p] = to_own(tnw[2, x, p])
+            put_ends(2, edge[0], edge[7], edge[0], tew[2, 7, p], p, 3)
         to_rows(s, pm, yp, po)
 
         @pl.when((s == 0) & first_to_above)
@@ -705,29 +720,30 @@
         def _():
             low_send.start()
 
-        def balance(k, inner):
+        def balance(i, inner):
+            k = lax.rem(i + 2, 3)
             val = [[pm[k, x, p] for p in range(2)] for x in range(8)]
             f_e = [[None, None] for _ in range(8)]
             for x in range(8):
                 for p in range(2):
-                    east_v = val[x + 1][p] if x < 7 else lane_roll(val[0][p], -1)
+                    east_v = val[x + 1][p] if x < 7 else ends[k, 0, p]
                     f_e[x][p] = tem[k, x, p] * (val[x][p] - east_v)
             for x in range(8):
-                after = lane_roll(jnp.where(lower, pm[k + 1, x, 0], val[x][0]), 4)
+                after = lane_roll(jnp.where(slot_of == 0, pm[i, x, 0], val[x][0]), -2)
                 after = sub_roll(jnp.where(row0, after, val[x][0]), -1)
                 f_n0 = tnm[k, x, 0] * (val[x][0] - val[x][1])
                 f_n1 = tnm[k, x, 1] * (val[x][1] - after)
-                before = lane_roll(jnp.where(lower, f_n1, pu[x]), 4)
+                before = lane_roll(jnp.where(slot_of == 3, pu[x], f_n1), 2)
                 before = sub_roll(jnp.where(row7, before, f_n1), 1)
                 pu[x] = f_n1
                 f_n = (f_n0, f_n1)
                 f_s = (before, f_n0)
                 for p in range(2):
-                    f_w = f_e[x - 1][p] if x else lane_roll(f_e[7][p], 1)
+                    f_w = f_e[x - 1][p] if x else jnp.where(even, lane_roll(f_e[7][p], -1), ends[k, 1, p])
                     hm[k, x, p] = (f_e[x][p] - f_w) + (f_n[p] - f_s[p])
             return inner
 
-        lax.fori_loop(0, 5, balance, 0)
+        lax.fori_loop(0, 3, balance, 0)
         to_rows(s, hm, yh, ro)
         return carry
 
@@ -819,8 +835,8 @@
             vmem(3, 8, 2, 8, 128),
             vmem(3, 8, 2, 8, 128),
             vmem(3, 3, 8, 2, 8, 128),
-            vmem(5, 8, 2, 8, 128),
-            vmem(5, 8, 2, 8, 128),
+            vmem(3, 8, 2, 8, 128),
+            vmem(3, 8, 2, 8, 128),
             vmem(4, 8, 2, 8, 128),
             vmem(3, 8, 2, 8, 128),
             vmem(2, 14, 8, 128),
@@ -828,8 +844,9 @@
             vmem(2, 3, 8, 128),
             vmem(5, 4, 8, 128),
             vmem(8, 8, 128),
-            vmem(6, 8, 2, 8, 128),
-            vmem(5, 8, 2, 8, 128),
+            vmem(3, 2, 2, 8, 128),
+            vmem(3, 8, 2, 8, 128),
+            vmem(3, 8, 2, 8, 128),
             vmem(2, 144, 128),
             vmem(2, 144, 128),
             vmem(512, 128),

time: 29.8 us -> 29.4 us (0.987)
  Pallas kernels: 27.6 us -> 27.3 us
    pallas_call x1, Pallas kernels: 27.6 us -> 27.3 us  [body(): pl.pallas_call(kernel, out_shape=[jax.ShapeDtypeStruct((512, 128), F32)]...]
where the time goes in v4:
time: 29.4 us; the launch traced here: 29.3 us
  Pallas kernels  27.3 us (93%)
  local copies, waits for them, and re-layouts  1.41 us (5%)
  between operations  0.64 us (2%)
    pallas_call x1, Pallas kernels, body(): pl.pallas_call(kernel, out_shape=[jax.ShapeDtypeStruct((512, 128), F32)]...  27.3 us
    unnamed x2, local copies, waits for them, and re-layouts  1.41 us

profile of v4, /device:TPU:25, one launch (start us, length us, event | category | flops | bytes accessed | tf_op | source)
XLA Modules:
  0.0 29.3 jit_solution(1942019654643197379)
XLA Ops:
  0.6 27.3 %shard_map.59 = (f32[512,128]{1,0:T(8,128)S(1)}, f32[512,128]{1,0:T(8,128)S(1)}) custom-call(f32[32,2,8,128]{3,2,1,0:T(8,128)} %bitcast.8, f32[32,2,8,128]{3,2,1,0:T(8,128)} %bitcast.9, f32[32,2,8,128]{3,2,1,0:T(8,128)} %bitcast.10, f32[512,128]{1,0:T(8,128)} %bitcast.11), custom_call_target="tpu_custom_call" | custom-call | tf_op jit(solution)/shard_map/pallas_call | solution.py:807
  27.9 0.7 %copy.8 = f32[32,16,128]{2,1,0:T(8,128)} copy(f32[32,16,128]{2,1,0:T(8,128)S(1)} %bitcast.7) | data formatting | bytes 524288
  28.6 0.7 %copy.9 = f32[32,16,128]{2,1,0:T(8,128)} copy(f32[32,16,128]{2,1,0:T(8,128)S(1)} %bitcast.6) | data formatting | bytes 524288

commit v5 on v4

--- a/solution.py
+++ b/solution.py
@@ -796,6 +796,17 @@
         copy.start()
     middle_copy.wait()
     for copy in edge_copies:
+        copy.wait()
+
+
+def flush(press, resid, press_out, resid_out, sem):
+    copies = [
+        pltpu.make_async_copy(press, press_out, sem.at[0]),
+        pltpu.make_async_copy(resid, resid_out, sem.at[1]),
+    ]
+    for copy in copies:
+        copy.start()
+    for copy in copies:
         copy.wait()
 
 
@@ -877,6 +888,14 @@
             )
         ),
     )
+    pressure, residual = pl.pallas_call(
+        flush,
+        out_shape=[jax.ShapeDtypeStruct((512, 128), F32)] * 2,
+        in_specs=[anywhere] * 2,
+        out_specs=[anywhere] * 2,
+        scratch_shapes=[pltpu.SemaphoreType.DMA((2,))],
+        compiler_params=pltpu.CompilerParams(vmem_limit_bytes=1024 * 1024),
+    )(pressure, residual)
     return pressure.reshape(32, 16, 128), residual.reshape(32, 16, 128)
 
 

time: 29.4 us -> 28.8 us (0.980)
  local copies, waits for them, and re-layouts: 1.41 us -> 0 us
  Pallas kernels: 27.3 us -> 28.1 us
    unnamed x2 -> x0, local copies, waits for them, and re-layouts: 1.41 us -> none
    pallas_call x0 -> x1, Pallas kernels: none -> 0.81 us  [body(): pl.pallas_call(flush, out_shape=[jax.ShapeDtypeStruct((512, 128), F32)] *...]
where the time goes in v5:
time: 28.8 us; the launch traced here: 28.7 us
  Pallas kernels  28.1 us (98%)
  between operations  0.64 us (2%)
    pallas_call x1, Pallas kernels, body(): pl.pallas_call(kernel, out_shape=[jax.ShapeDtypeStruct((512, 128), F32)]...  27.3 us
    pallas_call x1, Pallas kernels, body(): pl.pallas_call(flush, out_shape=[jax.ShapeDtypeStruct((512, 128), F32)] *...  0.81 us

profile of v5, /device:TPU:25, one launch (start us, length us, event | category | flops | bytes accessed | tf_op | source)
XLA Modules:
  0.0 28.7 jit_solution(262384489119005153)
XLA Ops:
  0.6 27.3 %shard_map.59 = (f32[512,128]{1,0:T(8,128)S(1)}, f32[512,128]{1,0:T(8,128)S(1)}) custom-call(f32[32,2,8,128]{3,2,1,0:T(8,128)} %bitcast.6, f32[32,2,8,128]{3,2,1,0:T(8,128)} %bitcast.7, f32[32,2,8,128]{3,2,1,0:T(8,128)} %bitcast.8, f32[512,128]{1,0:T(8,128)} %bitcast.9), custom_call_target="tpu_custom_call" | custom-call | tf_op jit(solution)/shard_map/pallas_call | solution.py:818
  27.9 0.8 %shard_map.60 = (f32[512,128]{1,0:T(8,128)}, f32[512,128]{1,0:T(8,128)}) custom-call(f32[512,128]{1,0:T(8,128)S(1)} %get-tuple-element.6.press, f32[512,128]{1,0:T(8,128)S(1)} %get-tuple-element.7.resid), custom_call_target="tpu_custom_call" | custom-call | tf_op jit(solution)/shard_map/pallas_call | solution.py:891

commit v6 on v5

--- a/solution.py
+++ b/solution.py
@@ -458,7 +458,7 @@
             value = value + sub_roll(value, 1)
             sums[e, index] = value + lane_roll(value, -1)
 
-    def owned(s, carry):
+    def owned(s):
         copies = halo(s, 0, 7)
         copies[0].wait_recv()
         copies[1].wait_recv()
@@ -477,7 +477,7 @@
             if x < 8:
                 value = turn(hx_rows, 512 + 128 * s + x, 768 + 128 * s + x)
             else:
-                value = turn(hx_rows, 768 + 128 * s, None, row24[pl.ds(pl.multiple_of(16 * s, 16), 16), :])
+                value = turn(hx_rows, 768 + 128 * s, None, row24[pl.ds(16 * s, 16), :])
             tp[1, x, pl.ds(8, 128), :] = value
             first_rows[s, x] = value[:16]
         for copy in copies[2:5]:
@@ -501,8 +501,9 @@
 
         lax.fori_loop(0, 2, unit, 0)
 
-        copies[5].wait_recv()
-        copies[6].wait_recv()
+    def coarse_sums(s):
+        for copy in halo(s, 5, 7):
+            copy.wait_recv()
         for rows, turned, at_row in ((ax_rows, ta, 16), (sx_rows, ts, 24)):
             for x in range(8):
                 turned[x, pl.ds(0, 128), :] = turn(rows, 256 + 128 * s + x, 512 + 128 * s + x)
@@ -527,9 +528,6 @@
             ga[s, 0, m] = packed
         for copy in sums_messages(s):
             copy.start()
-        return carry
-
-    lax.fori_loop(0, SETS, owned, 0)
 
     even = group % 2 == 0
     even_slot = slot_of % 2 == 0
@@ -560,7 +558,7 @@
                 for half in range(2):
                     for b in range(2):
                         first = 32 * q + 16 * (1 - half) + 8 * b
-                        layer = lax.rem(16 * s + (8 * b + 24), LAYERS)
+                        layer = (16 * s + 8 * b + 24) % LAYERS
                         dst[pl.ds(16 * layer + (8 * half + 4 * part + q), 8, stride=16), :] = turned[first : first + 8]
 
     low_send = pltpu.make_async_remote_copy(
@@ -576,7 +574,7 @@
         device_id=peer(0, 0, 1), device_id_type=MESH,
     )
 
-    def rest(s, carry):
+    def others(s):
         for copy in halo(s, 7):
             copy.wait_recv()
         for x in range(9):
@@ -612,6 +610,7 @@
             return inner
 
         lax.fori_loop(0, 3, unit, 0)
+    def solution_of(s):
         for copy in sums_messages(s):
             copy.wait()
         table = []
@@ -720,6 +719,7 @@
         def _():
             low_send.start()
 
+    def fluxes(s):
         def balance(i, inner):
             k = lax.rem(i + 2, 3)
             val = [[pm[k, x, p] for p in range(2)] for x in range(8)]
@@ -745,9 +745,20 @@
 
         lax.fori_loop(0, 3, balance, 0)
         to_rows(s, hm, yh, ro)
-        return carry
-
-    lax.fori_loop(0, SETS, rest, 0)
+
+    owned(0)
+    coarse_sums(0)
+    others(0)
+    owned(1)
+    solution_of(0)
+    coarse_sums(1)
+    fluxes(0)
+    others(1)
+    for s in range(SETS):
+        for copy in halo(s):
+            copy.wait_send()
+    solution_of(1)
+    fluxes(1)
     press_copy = pltpu.make_async_copy(po, press_out, out_sem.at[0])
     press_copy.start()
 
@@ -767,9 +778,6 @@
 
     middle_copy = pltpu.make_async_copy(ro.at[pl.ds(16, 480)], resid_out.at[pl.ds(16, 480)], out_sem.at[1])
     middle_copy.start()
-    for s in range(SETS):
-        for copy in halo(s):
-            copy.wait_send()
     press_copy.wait()
 
     @pl.when(has_below)

time: 28.8 us -> 28.6 us (level)
  the two profiles are of different devices: /device:TPU:25 before, /device:TPU:1 now
where the time goes in v6:
time: 28.6 us; the launch traced here: 28.5 us
  Pallas kernels  27.9 us (98%)
  between operations  0.64 us (2%)
    pallas_call x1, Pallas kernels, body(): pl.pallas_call(kernel, out_shape=[jax.ShapeDtypeStruct((512, 128), F32)]...  27.1 us
    pallas_call x1, Pallas kernels, body(): pl.pallas_call(flush, out_shape=[jax.ShapeDtypeStruct((512, 128), F32)] *...  0.81 us

profile of v6, /device:TPU:1, one launch (start us, length us, event | category | flops | bytes accessed | tf_op | source)
XLA Modules:
  0.0 28.5 jit_solution(12641429068605745074)
XLA Ops:
  0.6 27.1 %shard_map.59 = (f32[512,128]{1,0:T(8,128)S(1)}, f32[512,128]{1,0:T(8,128)S(1)}) custom-call(f32[32,2,8,128]{3,2,1,0:T(8,128)} %bitcast.6, f32[32,2,8,128]{3,2,1,0:T(8,128)} %bitcast.7, f32[32,2,8,128]{3,2,1,0:T(8,128)} %bitcast.8, f32[512,128]{1,0:T(8,128)} %bitcast.9), custom_call_target="tpu_custom_call" | custom-call | tf_op jit(solution)/shard_map/pallas_call | solution.py:826
  27.7 0.8 %shard_map.60 = (f32[512,128]{1,0:T(8,128)}, f32[512,128]{1,0:T(8,128)}) custom-call(f32[512,128]{1,0:T(8,128)S(1)} %get-tuple-element.6.press, f32[512,128]{1,0:T(8,128)S(1)} %get-tuple-element.7.resid), custom_call_target="tpu_custom_call" | custom-call | tf_op jit(solution)/shard_map/pallas_call | solution.py:899
